TPU v7x, 256 devices: a whole 4x4x8 slice. The times are simulated.
256 devices in a mesh: row: 32 (over x, z), col: 8 (over y, core).
Axes of the slice: x: 4, y: 4, z: 8, core: 2. Of those that a mesh axis runs over, the one named last changes fastest.
Arguments:
- blocks: bfloat16 [32, 8, 256, 128, 128], P('row', 'col'), may hold values from -0.1875 to 0.1875
- block_rows: int32 [32, 8, 256], P('row', 'col'), may hold values from 0 to 255
- block_cols: int32 [32, 8, 256], P('row', 'col'), may hold values from 0 to 255
- counts: int32 [32, 8], P('row', 'col'), may hold values from 85 to 256, as said below
- data: float32 [1048576], P('row'), may hold values from -16 to 16
Outputs:
- solution: float32 [262144], P('col')
- search: float32 [262144], P('col')
- data_basis: float32 [1048576], P('row')
Inputs may be any that keep to these rules, and one draw needn't show every extreme that they name: `counts`: every tile has between 85 and 256 live slots; some tile has exactly 256.
All inputs are finite; a program needn't handle non-finite values.
Results may differ from a plain program's by a relative error of at most 0.013.
Values sent between devices are 32-bit elements; how exact they have to be, the bound alone decides.
A program may use at most 64 MiB of HBM per device.

v0:
```python
import jax
import jax.numpy as jnp
from jax import lax
from jax.sharding import PartitionSpec as P

TILE_COLS = 256
ITERS = 3


EPS = 1e-06


def local_forward(tile_blocks, rows, cols, count, vector, tile_rows):
    width = tile_blocks.shape[-1]
    vec_b = vector.astype(jnp.bfloat16).reshape(-1, width)
    picked = jnp.take(vec_b, cols, axis=0)
    prod = jnp.einsum("kij,kj->ki", tile_blocks, picked, preferred_element_type=jnp.float32)
    live = (jnp.arange(tile_blocks.shape[0], dtype=jnp.int32) < count).astype(jnp.float32)
    prod = prod * live[:, None]
    return jax.ops.segment_sum(prod, rows, num_segments=tile_rows).reshape(-1)


def local_adjoint(tile_blocks, rows, cols, count, vector, tile_cols):
    width = tile_blocks.shape[-1]
    vec_b = vector.astype(jnp.bfloat16).reshape(-1, width)
    picked = jnp.take(vec_b, rows, axis=0)
    prod = jnp.einsum("kij,ki->kj", tile_blocks, picked, preferred_element_type=jnp.float32)
    live = (jnp.arange(tile_blocks.shape[0], dtype=jnp.int32) < count).astype(jnp.float32)
    prod = prod * live[:, None]
    return jax.ops.segment_sum(prod, cols, num_segments=tile_cols).reshape(-1)


def first_norm(data):
    return jnp.sqrt(lax.psum(jnp.sum(data * data), "row") + EPS)


def new_data_basis(partial_value, previous, alpha):
    summed = lax.psum(partial_value, "col")
    temp = summed - alpha * previous
    return (temp, None)


def new_model_basis(partial_value, previous, beta):
    summed = lax.psum(partial_value, "row")
    temp = summed - beta * previous
    alpha = jnp.sqrt(lax.psum(jnp.sum(temp * temp), "col") + EPS)
    return (temp / alpha, alpha)


def per_device(blocks, block_rows, block_cols, counts, data):
    tile_blocks = blocks[0, 0]
    rows = block_rows[0, 0]
    cols = block_cols[0, 0]
    count = counts[0, 0]
    width = tile_blocks.shape[-1]
    tile_rows = data.shape[0] // width
    tile_cols = TILE_COLS
    beta = first_norm(data)
    data_basis = data / beta
    zero_model = jnp.zeros((tile_cols * width,), jnp.float32)
    model_basis, alpha = new_model_basis(
        local_adjoint(tile_blocks, rows, cols, count, data_basis, tile_cols),
        zero_model,
        jnp.float32(0.0),
    )
    search = model_basis
    solution = zero_model
    phibar = beta
    rhobar = alpha
    for step in range(ITERS):
        partial_value = local_forward(tile_blocks, rows, cols, count, model_basis, tile_rows)
        temp, unused = new_data_basis(partial_value, data_basis, alpha)
        beta = first_norm(temp)
        data_basis = temp / beta
        partial_model = local_adjoint(tile_blocks, rows, cols, count, data_basis, tile_cols)
        model_basis, alpha = new_model_basis(partial_model, model_basis, beta)
        rho = jnp.sqrt(rhobar * rhobar + beta * beta)
        cosine = rhobar / rho
        sine = beta / rho
        theta = sine * alpha
        rhobar = -cosine * alpha
        phi = cosine * phibar
        phibar = sine * phibar
        solution = solution + phi / rho * search
        search = model_basis - theta / rho * search
    return (solution, search, data_basis)


def solution(mesh):
    in_specs = (
        P("row", "col", None, None, None),
        P("row", "col", None),
        P("row", "col", None),
        P("row", "col"),
        P("row"),
    )
    out_specs = (P("col"), P("col"), P("row"))
    return jax.shard_map(
        per_device, mesh=mesh, in_specs=in_specs, out_specs=out_specs, check_vma=False
    )
```

profile of v0, /device:TPU:1, one launch (start us, length us, event | category | flops | bytes accessed | tf_op | source)
XLA Modules:
  0.0 1181.6 jit_solution(13351661492889106659)
XLA Ops:
  8.6 1.5 multiply_reduce_fusion.7
  10.8 65.0 %psum.105 = f32[]{:T(128)} all-reduce(f32[]{:T(128)} %multiply_reduce_fusion.7), channel_id=1, replica_groups=mesh['row'=32,'col'=8] {'row'}, use_global_device_ids=true, to_apply=%region_1.0 | all-reduce | flops 1 | bytes 8 | tf_op jit(solution)/shard_map/psum | solution.py:34
  76.5 0.9 convert_bitcast_fusion.6
  77.4 0.9 gather_fusion
  78.4 5.7 fusion.12
  84.1 2.1 scatter_custom_fusion
  86.3 145.1 %all-reduce.8.cloned.1.call-done = f32[32768]{0:T(1024)} async-done(((f32[32768]{0:T(1024)}), f32[32768]{0:T(1024)}) %all-reduce.8.cloned.1.call-update) | async-done | bytes 131088 | tf_op jit(solution)/shard_map/psum | solution.py:44
  231.4 1.5 multiply_reduce_fusion.6
  233.0 16.8 %psum.107 = f32[]{:T(128)} all-reduce(f32[]{:T(128)} %multiply_reduce_fusion.6), channel_id=1, replica_groups=mesh['row'=32,'col'=8] {'col'}, use_global_device_ids=true, to_apply=%region_5.7 | all-reduce | flops 1 | bytes 8 | tf_op jit(solution)/shard_map/psum | solution.py:46
  250.5 0.9 convert_bitcast_fusion.5
  251.4 0.9 gather_fusion.1
  252.4 7.8 fusion.10
  260.2 2.3 scatter_custom_fusion.1
  262.6 58.5 %all-reduce.10.cloned.1.call-done = f32[32768]{0:T(1024)} async-done(((f32[32768]{0:T(1024)}), f32[32768]{0:T(1024)}) %all-reduce.10.cloned.1.call-update) | async-done | bytes 131088 | tf_op jit(solution)/shard_map/psum | solution.py:38
  321.1 1.6 multiply_reduce_fusion.5
  322.6 61.7 %psum.109 = f32[]{:T(128)} all-reduce(f32[]{:T(128)} %get-tuple-element.10), channel_id=1, replica_groups=mesh['row'=32,'col'=8] {'row'}, use_global_device_ids=true, to_apply=%region_9.11 | all-reduce | flops 1 | bytes 8 | tf_op jit(solution)/shard_map/psum | solution.py:34
  385.1 0.9 gather_fusion.2
  386.0 5.7 fusion.8
  391.7 2.1 scatter_custom_fusion.2
  393.9 144.3 %all-reduce.12.cloned.1.call-done = f32[32768]{0:T(1024)} async-done(((f32[32768]{0:T(1024)}), f32[32768]{0:T(1024)}) %all-reduce.12.cloned.1.call-update) | async-done | bytes 131088 | tf_op jit(solution)/shard_map/psum | solution.py:44
  538.2 1.6 multiply_reduce_fusion.4
  539.8 17.0 %psum.111 = f32[]{:T(128)} all-reduce(f32[]{:T(128)} %multiply_reduce_fusion.4), channel_id=1, replica_groups=mesh['row'=32,'col'=8] {'col'}, use_global_device_ids=true, to_apply=%region_13.15 | all-reduce | flops 1 | bytes 8 | tf_op jit(solution)/shard_map/psum | solution.py:46
  557.5 0.9 convert_bitcast_fusion.3
  558.4 0.9 gather_fusion.3
  559.4 7.8 fusion.6
  567.2 2.3 scatter_custom_fusion.3
  569.5 58.5 %all-reduce.14.cloned.1.call-done = f32[32768]{0:T(1024)} async-done(((f32[32768]{0:T(1024)}), f32[32768]{0:T(1024)}) %all-reduce.14.cloned.1.call-update) | async-done | bytes 131088 | tf_op jit(solution)/shard_map/psum | solution.py:38
  628.1 1.5 multiply_reduce_fusion.3
  629.6 61.7 %psum.113 = f32[]{:T(128)} all-reduce(f32[]{:T(128)} %get-tuple-element.6), channel_id=1, replica_groups=mesh['row'=32,'col'=8] {'row'}, use_global_device_ids=true, to_apply=%region_17.19 | all-reduce | flops 1 | bytes 8 | tf_op jit(solution)/shard_map/psum | solution.py:34
  693.0 5.7 fusion.4
  698.6 2.1 scatter_custom_fusion.4
  700.9 144.4 %all-reduce.16.cloned.1.call-done = f32[32768]{0:T(1024)} async-done(((f32[32768]{0:T(1024)}), f32[32768]{0:T(1024)}) %all-reduce.16.cloned.1.call-update) | async-done | bytes 131088 | tf_op jit(solution)/shard_map/psum | solution.py:44
  845.3 1.5 multiply_reduce_fusion.2
  846.8 16.8 %psum.115 = f32[]{:T(128)} all-reduce(f32[]{:T(128)} %multiply_reduce_fusion.2), channel_id=1, replica_groups=mesh['row'=32,'col'=8] {'col'}, use_global_device_ids=true, to_apply=%region_21.23 | all-reduce | flops 1 | bytes 8 | tf_op jit(solution)/shard_map/psum | solution.py:46
  864.3 0.9 convert_bitcast_fusion.1
  865.2 0.9 gather_fusion.5
  866.2 7.8 fusion.2
  874.0 2.3 scatter_custom_fusion.5
  876.4 58.5 %all-reduce.18.cloned.1.call-done = f32[32768]{0:T(1024)} async-done(((f32[32768]{0:T(1024)}), f32[32768]{0:T(1024)}) %all-reduce.18.cloned.1.call-update) | async-done | bytes 131088 | tf_op jit(solution)/shard_map/psum | solution.py:38
  934.9 1.5 multiply_reduce_fusion.1
  936.5 61.9 %psum.117 = f32[]{:T(128)} all-reduce(f32[]{:T(128)} %multiply_reduce_fusion.1), channel_id=1, replica_groups=mesh['row'=32,'col'=8] {'row'}, use_global_device_ids=true, to_apply=%region_25.27 | all-reduce | flops 1 | bytes 8 | tf_op jit(solution)/shard_map/psum | solution.py:34
  999.1 1.6 convert_bitcast_fusion
  1001.6 5.7 fusion
  1007.3 2.1 scatter_custom_fusion.6
  1010.0 143.8 %all-reduce.20.cloned.1.call-done = f32[32768]{0:T(1024)} async-done(((f32[32768]{0:T(1024)}), f32[32768]{0:T(1024)}) %all-reduce.20.cloned.1.call-update) | async-done | bytes 131088 | tf_op jit(solution)/shard_map/psum | solution.py:44
  1153.8 1.6 multiply_reduce_fusion
  1155.4 16.8 %psum.119 = f32[]{:T(128)} all-reduce(f32[]{:T(128)} %multiply_reduce_fusion), channel_id=1, replica_groups=mesh['row'=32,'col'=8] {'col'}, use_global_device_ids=true, to_apply=%region_29.31 | all-reduce | flops 1 | bytes 8 | tf_op jit(solution)/shard_map/psum | solution.py:46
  1173.0 1.7 multiply_subtract_fusion
  (40 shorter events, 4.3 us)
Async XLA Ops:
  7.2 76.9 %copy-start.3 = (s32[1,1,256]{2,1,0:T(1,128)S(1)}, s32[1,1,256]{2,1,0:T(1,128)}, u32[]{:S(2)}) copy-start(s32[1,1,256]{2,1,0:T(1,128)} %param.9) | copy-start | bytes 3076
  7.2 224.3 %all-reduce.8.cloned.1.call-start = ((), (), s32[]{:S(2)}) async-start(), calls=%async_computation | async-start | bytes 262144 | tf_op jit(solution)/shard_map/psum | solution.py:44
  78.4 242.7 %copy-start.2 = (f32[32768]{0:T(1024)S(1)}, f32[32768]{0:T(1024)}, u32[]{:S(2)}) copy-start(f32[32768]{0:T(1024)} %param.11) | copy-start | bytes 393220
  86.2 234.8 %all-reduce.10.cloned.1.call-start = ((), (), s32[]{:S(2)}) async-start(), calls=%async_computation.1 | async-start | bytes 262144 | tf_op jit(solution)/shard_map/psum | solution.py:38
  252.4 285.9 %copy-start = (f32[32768]{0:T(1024)S(1)}, f32[32768]{0:T(1024)}, u32[]{:S(2)}) copy-start(f32[32768]{0:T(1024)} %all-reduce.8.cloned.1.call-done) | copy-start | bytes 393220
  262.5 275.7 %all-reduce.12.cloned.1.call-start = ((), (), s32[]{:S(2)}) async-start(), calls=%async_computation.2 | async-start | bytes 262144 | tf_op jit(solution)/shard_map/psum | solution.py:44
  393.9 234.2 %all-reduce.14.cloned.1.call-start = ((), (), s32[]{:S(2)}) async-start(), calls=%async_computation.3 | async-start | bytes 262144 | tf_op jit(solution)/shard_map/psum | solution.py:38
  569.5 275.8 %all-reduce.16.cloned.1.call-start = ((), (), s32[]{:S(2)}) async-start(), calls=%async_computation.4 | async-start | bytes 262144 | tf_op jit(solution)/shard_map/psum | solution.py:44
  700.8 234.1 %all-reduce.18.cloned.1.call-start = ((), (), s32[]{:S(2)}) async-start(), calls=%async_computation.5 | async-start | bytes 262144 | tf_op jit(solution)/shard_map/psum | solution.py:38
  866.2 287.6 %copy-start.1 = (f32[32768]{0:T(1024)S(1)}, f32[32768]{0:T(1024)}, u32[]{:S(2)}) copy-start(f32[32768]{0:T(1024)} %all-reduce.16.cloned.1.call-done) | copy-start | bytes 393220
  876.3 277.5 %all-reduce.20.cloned.1.call-start = ((), (), s32[]{:S(2)}) async-start(), calls=%async_computation.6 | async-start | bytes 262144 | tf_op jit(solution)/shard_map/psum | solution.py:44
Sparse Core Ops, SparseCore 0:
  86.4 145.0 all-reduce.7
  262.6 58.4 all-reduce.9
  394.0 144.2 all-reduce.11
  569.6 58.3 all-reduce.13
  700.9 144.2 all-reduce.15
  876.5 58.4 all-reduce.17
  1009.6 144.2 all-reduce.19
where the time goes:
time: 1180 us
  waiting for transfers between devices  753 us (64%)
  blocking collectives  318 us (27%)
  matrix products  46 us (4%)
  other arithmetic  37 us (3%)
  between operations  21.2 us (2%)
    psum x4, waiting for transfers between devices, new_model_basis(): summed = lax.psum(partial_value, 'row')  578 us
    psum x4, blocking collectives, first_norm(): return jnp.sqrt(lax.psum(jnp.sum(data * data), 'row') + EPS)  250 us
    psum x3, waiting for transfers between devices, new_data_basis(): summed = lax.psum(partial_value, 'col')  176 us
    psum x4, blocking collectives, new_model_basis(): alpha = jnp.sqrt(lax.psum(jnp.sum(temp * temp), 'col') + EPS)  67.4 us
  transfers between devices with their start and end apart: 7, of which 7 were waited for; matrix products, arithmetic and copies ran while one was open for 0% of the time, Pallas kernels for 0%

commit v1 on v0

v1 whole, which is shorter than its diff:
```python
import jax
import jax.numpy as jnp
from jax import lax
from jax.experimental import pallas as pl
from jax.experimental.pallas import tpu as pltpu
from jax.sharding import PartitionSpec as P

MESH = pl.DeviceIdType.MESH
F32 = jnp.float32
BF16 = jnp.bfloat16
EPS = 1e-06
ITERS = 3
B = 128
NB = 256
NX, NZ, NY, NC = 4, 8, 4, 2
N_ROW = NX * NZ
N_COL = NY * NC
RCH = NB // N_ROW
CCH = NB // N_COL
GROUP = 16


def ring(step, size):
    return min(step, size - step)


ROW_STEPS = sorted(
    ((dx, dz) for dx in range(NX) for dz in range(NZ) if dx or dz),
    key=lambda s: -(ring(s[0], NX) + ring(s[1], NZ)),
)
COL_STEPS = sorted(
    ((dy, dc) for dy in range(NY) for dc in range(NC) if dy or dc),
    key=lambda s: -(2 * ring(s[0], NY) + s[1]),
)


def block_products(blocks_ref, picks, out_ref):
    row = lax.broadcasted_iota(jnp.int32, (GROUP, B), 0)
    half = GROUP // 2
    for g in range(NB // GROUP):
        base = g * GROUP
        mine = picks[base : base + GROUP]
        lhs = jnp.concatenate(
            [jnp.where((row & (half - 1)) == q, mine, 0.0).astype(BF16) for q in range(half)], axis=1
        )
        left = jnp.concatenate([blocks_ref[base + q] for q in range(half)], axis=0)
        right = jnp.concatenate([blocks_ref[base + half + q] for q in range(half)], axis=0)
        rhs = jnp.concatenate([left, right], axis=1)
        res = jnp.dot(lhs, rhs, preferred_element_type=F32)
        out_ref[base : base + GROUP, :] = jnp.where(row < half, res[:, :B], res[:, B:])


def pick_rows(pick, vector):
    return jnp.dot(pick, vector.astype(BF16), preferred_element_type=F32)


def scatter_rows(place, prod):
    high = prod.astype(BF16)
    low = (prod - high.astype(F32)).astype(BF16)
    return jnp.dot(place, high, preferred_element_type=F32) + jnp.dot(
        place, low, preferred_element_type=F32
    )


def lane_squares(vector):
    return jnp.sum(vector * vector, axis=0, keepdims=True)


def norm_of(parts):
    return jnp.sqrt(jnp.sum(parts, axis=(0, 1), keepdims=True) + EPS)


def kernel(
    blocks_hbm, rows_hbm, cols_hbm, counts_ref, data_hbm,
    sol_ref, search_ref, basis_ref,
    blk, blk_t, rows_v, cols_v, pick_r, pick_c, place_r, place_c, prod,
    tb, wb, gsend, grecv, fsend, frecv, asend, arecv, scal,
    in_sem, blk_sem, g_ssem, g_rsem, w_ssem, w_rsem, f_ssem, f_rsem, t_ssem, t_rsem, a_ssem, a_rsem,
):
    r = lax.axis_index("row")
    c = lax.axis_index("col")
    x, z = r // NZ, r % NZ
    y, core = c // NC, c % NC
    row_peers = [((x + dx) % NX) * NZ + (z + dz) % NZ for dx, dz in ROW_STEPS]
    col_peers = [((y + dy) % NY) * NC + (core + dc) % NC for dy, dc in COL_STEPS]

    barrier = pltpu.get_barrier_semaphore()
    for p in row_peers:
        pl.semaphore_signal(barrier, inc=1, device_id=(p, c), device_id_type=MESH)
    for p in col_peers:
        pl.semaphore_signal(barrier, inc=1, device_id=(r, p), device_id_type=MESH)

    small = [
        pltpu.make_async_copy(rows_hbm, rows_v, in_sem.at[0]),
        pltpu.make_async_copy(cols_hbm, cols_v, in_sem.at[1]),
        pltpu.make_async_copy(data_hbm, tb.at[0], in_sem.at[2]),
    ]
    for copy in small:
        copy.start()
    big = pltpu.make_async_copy(blocks_hbm.at[0, 0], blk, blk_sem)
    big.start()
    for copy in small:
        copy.wait()

    count = counts_ref[0, 0]
    sub = lax.broadcasted_iota(jnp.int32, (NB, NB), 0)
    lane = lax.broadcasted_iota(jnp.int32, (NB, NB), 1)
    live = lane < count

    def one_hot(index_ref):
        return (sub == index_ref[...]).astype(F32)

    hot_r = one_hot(rows_v)
    pick_r[...] = hot_r.T.astype(BF16)
    place_r[...] = jnp.where(live, hot_r, 0.0).astype(BF16)
    hot_c = one_hot(cols_v)
    pick_c[...] = hot_c.T.astype(BF16)
    place_c[...] = jnp.where(live, hot_c, 0.0).astype(BF16)
    big.wait()

    def adjoint_part(it):
        vec = tb[it]
        block_products(blk, pick_rows(pick_r[...], vec), prod)
        part = scatter_rows(place_c[...], prod[...])
        gsend[:, :RCH, :] = part.reshape(N_ROW, RCH, B)
        gsend[:, RCH:, :] = jnp.broadcast_to(lane_squares(vec).reshape(1, 1, B), (N_ROW, 1, B))

    def start_adjoint_send(it):
        for j, p in enumerate(row_peers):
            pltpu.make_async_remote_copy(
                gsend.at[p], grecv.at[it, j], g_ssem, g_rsem.at[it], device_id=(p, c), device_id_type=MESH
            ).start()

    def finish_adjoint(it, first):
        got = grecv.at[it, pl.ds(0, N_ROW - 1)]
        pltpu.make_async_copy(got, got, g_rsem.at[it]).wait()
        total = jnp.sum(grecv[it, : N_ROW - 1], axis=0) + gsend[r]
        beta = norm_of(total[RCH:])
        chunk = total[:RCH] / beta
        if not first:
            alpha = scal[it - 1, 0:1, 0:1]
            chunk = chunk - beta * (wb[it - 1, r] / alpha)
        wb[it, r] = chunk
        scal[it, 1:2, :] = jnp.broadcast_to(beta, (1, B))
        for p in row_peers:
            pltpu.make_async_remote_copy(
                wb.at[it, r], wb.at[it, r], w_ssem, w_rsem.at[it], device_id=(p, c), device_id_type=MESH
            ).start()
        sent = gsend.at[pl.ds(0, N_ROW - 1)]
        pltpu.make_async_copy(sent, sent, g_ssem).wait()
        landed = wb.at[it, pl.ds(0, N_ROW - 1)]
        pltpu.make_async_copy(landed, landed, w_rsem.at[it]).wait()
        pltpu.make_async_copy(landed, landed, w_ssem).wait()

    def forward(it):
        vec = wb[it].reshape(NB, B)
        block_products(blk_t, pick_rows(pick_c[...], vec), prod)
        part = scatter_rows(place_r[...], prod[...])
        fsend[:, :CCH, :] = part.reshape(N_COL, CCH, B)
        fsend[:, CCH:, :] = jnp.broadcast_to(lane_squares(vec).reshape(1, 1, B), (N_COL, 1, B))
        for j, p in enumerate(col_peers):
            pltpu.make_async_remote_copy(
                fsend.at[p], frecv.at[it, j], f_ssem, f_rsem.at[it], device_id=(r, p), device_id_type=MESH
            ).start()
        got = frecv.at[it, pl.ds(0, N_COL - 1)]
        pltpu.make_async_copy(got, got, f_rsem.at[it]).wait()
        total = jnp.sum(frecv[it, : N_COL - 1], axis=0) + fsend[c]
        alpha = norm_of(total[CCH:])
        beta = scal[it, 1:2, 0:1]
        mine = pl.ds(pl.multiple_of(c * CCH, CCH), CCH)
        tb[it + 1, mine] = total[:CCH] / alpha - alpha * (tb[it, mine] / beta)
        scal[it, 0:1, :] = jnp.broadcast_to(alpha, (1, B))
        for p in col_peers:
            pltpu.make_async_remote_copy(
                tb.at[it + 1, mine], tb.at[it + 1, mine], t_ssem, t_rsem.at[it],
                device_id=(r, p), device_id_type=MESH,
            ).start()
        pltpu.make_async_copy(
            fsend.at[pl.ds(0, N_COL - 1)], fsend.at[pl.ds(0, N_COL - 1)], f_ssem
        ).wait()
        landed = tb.at[it + 1, pl.ds(0, NB - CCH)]
        pltpu.make_async_copy(landed, landed, t_rsem.at[it]).wait()
        pltpu.make_async_copy(landed, landed, t_ssem).wait()

    adjoint_part(0)
    pl.semaphore_wait(barrier, N_ROW + N_COL - 2)
    start_adjoint_send(0)

    def transpose_block(k, carry):
        blk_t[k] = blk[k].T
        return carry

    lax.fori_loop(0, NB, transpose_block, 0, unroll=8)
    finish_adjoint(0, True)

    def step(it, carry):
        forward(it)
        adjoint_part(it + 1)
        start_adjoint_send(it + 1)
        finish_adjoint(it + 1, False)
        return carry

    lax.fori_loop(0, ITERS, step, 0)

    asend[...] = lane_squares(wb[ITERS].reshape(NB, B))
    for j, p in enumerate(col_peers):
        pltpu.make_async_remote_copy(
            asend, arecv.at[j], a_ssem, a_rsem, device_id=(r, p), device_id_type=MESH
        ).start()

    alphas = [scal[i, 0:1, 0:1] for i in range(ITERS)]
    betas = [scal[i, 1:2, 0:1] for i in range(ITERS + 1)]
    basis_ref[...] = tb[ITERS] / betas[ITERS]
    search = wb[0].reshape(NB, B) / alphas[0]
    answer = jnp.zeros((NB, B), F32)
    phibar, rhobar = betas[0], alphas[0]
    for i in range(ITERS):
        beta = betas[i + 1]
        rho = jnp.sqrt(rhobar * rhobar + beta * beta)
        cosine, sine = rhobar / rho, beta / rho
        phi = cosine * phibar
        phibar = sine * phibar
        answer = answer + (phi / rho) * search
        if i + 1 < ITERS:
            theta = sine * alphas[i + 1]
            rhobar = -cosine * alphas[i + 1]
            search = wb[i + 1].reshape(NB, B) / alphas[i + 1] - (theta / rho) * search
    sol_ref[...] = answer
    pltpu.make_async_copy(arecv, arecv, a_rsem).wait()
    pltpu.make_async_copy(arecv, arecv, a_ssem).wait()
    squares = jnp.sum(arecv[...], axis=0) + asend[...]
    alpha = norm_of(squares)
    search_ref[...] = wb[ITERS].reshape(NB, B) / alpha - (sine * alpha / rho) * search


def per_device(blocks, block_rows, block_cols, counts, data):
    vec = jax.ShapeDtypeStruct((NB, B), F32)
    hbm = pl.BlockSpec(memory_space=pl.ANY)
    vmem = pl.BlockSpec(memory_space=pltpu.VMEM)
    sol, search, basis = pl.pallas_call(
        kernel,
        out_shape=(vec, vec, vec),
        in_specs=[hbm, hbm, hbm, pl.BlockSpec(memory_space=pltpu.SMEM), hbm],
        out_specs=(vmem, vmem, vmem),
        scratch_shapes=[
            pltpu.VMEM((NB, B, B), BF16),
            pltpu.VMEM((NB, B, B), BF16),
            pltpu.VMEM((1, NB), jnp.int32),
            pltpu.VMEM((1, NB), jnp.int32),
            pltpu.VMEM((NB, NB), BF16),
            pltpu.VMEM((NB, NB), BF16),
            pltpu.VMEM((NB, NB), BF16),
            pltpu.VMEM((NB, NB), BF16),
            pltpu.VMEM((NB, B), F32),
            pltpu.VMEM((ITERS + 1, NB, B), F32),
            pltpu.VMEM((ITERS + 1, N_ROW, RCH, B), F32),
            pltpu.VMEM((N_ROW, RCH + 1, B), F32),
            pltpu.VMEM((ITERS + 1, N_ROW, RCH + 1, B), F32),
            pltpu.VMEM((N_COL, CCH + 1, B), F32),
            pltpu.VMEM((ITERS, N_COL, CCH + 1, B), F32),
            pltpu.VMEM((1, B), F32),
            pltpu.VMEM((N_COL - 1, 1, B), F32),
            pltpu.VMEM((ITERS + 1, 8, B), F32),
            pltpu.SemaphoreType.DMA((3,)),
            pltpu.SemaphoreType.DMA,
            pltpu.SemaphoreType.DMA,
            pltpu.SemaphoreType.DMA((ITERS + 1,)),
            pltpu.SemaphoreType.DMA,
            pltpu.SemaphoreType.DMA((ITERS + 1,)),
            pltpu.SemaphoreType.DMA,
            pltpu.SemaphoreType.DMA((ITERS,)),
            pltpu.SemaphoreType.DMA,
            pltpu.SemaphoreType.DMA((ITERS,)),
            pltpu.SemaphoreType.DMA,
            pltpu.SemaphoreType.DMA,
        ],
        compiler_params=pltpu.CompilerParams(
            collective_id=0, has_side_effects=True, vmem_limit_bytes=48 * 1024 * 1024
        ),
        name="lsqr",
    )(blocks, block_rows[0], block_cols[0], counts, data.reshape(NB, B))
    return sol.reshape(-1), search.reshape(-1), basis.reshape(-1)


def solution(mesh):
    return jax.shard_map(
        per_device,
        mesh=mesh,
        in_specs=(
            P("row", "col", None, None, None),
            P("row", "col", None),
            P("row", "col", None),
            P("row", "col"),
            P("row"),
        ),
        out_specs=(P("col"), P("col"), P("row")),
        check_vma=False,
    )
```

time: 1180 us -> 104 us (0.09)
  waiting for transfers between devices: 753 us -> 0 us
  blocking collectives: 318 us -> 0 us
  Pallas kernels: 0 us -> 98.7 us
  matrix products: 46 us -> 0 us
  other arithmetic: 37 us -> 0 us
  between operations: 21.2 us -> 1.3 us
    psum x7 -> x0, waiting for transfers between devices: 753 us -> none  [the longest x4 578 us: new_model_basis(): summed = lax.psum(partial_value, 'row')]
    psum x8 -> x0, blocking collectives: 318 us -> none  [the longest x4 250 us: first_norm(): return jnp.sqrt(lax.psum(jnp.sum(data * data), 'row') + EPS)]
    pallas_call x0 -> x1, Pallas kernels: none -> 98.7 us  [per_device(): pl.pallas_call(kernel, out_shape=(vec, vec, vec), in_specs=[hbm, hbm, hbm...]
    dot_general x7 -> x0, matrix products: 46 us -> none  [the longest x3 23.4 us: local_forward(): jnp.einsum('kij,kj->ki', tile_blocks, picked, preferred_element_type=jnp....]
    scatter-add x7 -> x0, other arithmetic: 15.5 us -> none  [the longest x4 8.57 us: local_adjoint(): return jax.ops.segment_sum(prod, cols, num_segments=tile_cols).reshape(-1)]
    reduce_sum x8 -> x0, other arithmetic: 12.4 us -> none  [the longest x4 6.19 us: first_norm(): return jnp.sqrt(lax.psum(jnp.sum(data * data), 'row') + EPS)]
  transfers between devices with their start and end apart: 7 -> 0, of which waited for: 7 -> 0; matrix products, arithmetic and copies ran while one was open for 0% -> 0% of each run, Pallas kernels for 0% -> 0%
where the time goes in v1:
time: 104 us
  Pallas kernels  98.7 us (95%)
  local copies, waits for them, and re-layouts  4.25 us (4%)
  between operations  1.3 us (1%)
    pallas_call x1, Pallas kernels, per_device(): pl.pallas_call(kernel, out_shape=(vec, vec, vec), in_specs=[hbm, hbm, hbm...  98.7 us
    unnamed x9, local copies, waits for them, and re-layouts  4.25 us

profile of v1, /device:TPU:1, one launch (start us, length us, event | category | flops | bytes accessed | tf_op | source)
XLA Modules:
  0.0 104.3 jit_solution(11006315042453985975)
XLA Ops:
  1.3 0.0 copy-start
  1.3 0.9 copy-done
  2.2 0.0 copy-start.1
  2.2 0.7 copy-done.1
  2.9 0.0 copy-start.2
  2.9 0.7 copy-done.2
  3.5 98.7 %lsqr.1 = (f32[256,128]{1,0:T(8,128)S(1)}, f32[256,128]{1,0:T(8,128)S(1)}, f32[256,128]{1,0:T(8,128)S(1)}) custom-call(bf16[1,1,256,128,128]{4,3,2,1,0:T(8,128)(2,1)} %blocks_hbm.1, s32[1,256]{1,0:T(1,128)S(1)} %bitcast.10, s32[1,256]{1,0:T(1,128)S(1)} %bitcast.11, s32[1,1]{1,0:T(1,128)S(6)} %copy.11.counts_ref, f32[256,128]{1,0:T(8,128)S(1)} %bitcast.6), custom_call_target="tpu_custom_call" | custom-call | tf_op jit(solution)/shard_map/lsqr/pallas_call | solution.py:240
  102.3 0.7 copy.12
  102.9 0.7 copy.13
  103.6 0.7 copy.14
Async XLA Ops:
  1.3 0.9 copy-start
  2.2 0.7 copy-start.1
  2.9 0.7 copy-start.2

commit v2 on v1

--- a/solution.py
+++ b/solution.py
@@ -15,7 +15,9 @@
 NX, NZ, NY, NC = 4, 8, 4, 2
 N_ROW = NX * NZ
 N_COL = NY * NC
-RCH = NB // N_ROW
+OWN = N_ROW // 2
+RCH = NB // OWN
+LOADS = 4
 CCH = NB // N_COL
 GROUP = 16
 
@@ -28,17 +30,33 @@
     ((dx, dz) for dx in range(NX) for dz in range(NZ) if dx or dz),
     key=lambda s: -(ring(s[0], NX) + ring(s[1], NZ)),
 )
+
+
+def nearer(step):
+    other = ((step[0] + NX // 2) % NX, (step[1] + NZ // 2) % NZ)
+    mine = (ring(step[0], NX) + ring(step[1], NZ), step)
+    return mine < (ring(other[0], NX) + ring(other[1], NZ), other)
+
+
+SERVE_STEPS = [s for s in ROW_STEPS if nearer(s)]
 COL_STEPS = sorted(
     ((dy, dc) for dy in range(NY) for dc in range(NC) if dy or dc),
     key=lambda s: -(2 * ring(s[0], NY) + s[1]),
 )
 
 
-def block_products(blocks_ref, picks, out_ref):
+def chunk_of(x, z):
+    upper = x // (NX // 2)
+    return (x % (NX // 2)) * NZ + (z + upper * (NZ // 2)) % NZ
+
+
+def block_products(blocks_ref, picks, out_ref, loads=()):
     row = lax.broadcasted_iota(jnp.int32, (GROUP, B), 0)
     half = GROUP // 2
     for g in range(NB // GROUP):
         base = g * GROUP
+        if loads and base % (NB // LOADS) == 0:
+            loads[base * LOADS // NB].wait()
         mine = picks[base : base + GROUP]
         lhs = jnp.concatenate(
             [jnp.where((row & (half - 1)) == q, mine, 0.0).astype(BF16) for q in range(half)], axis=1
@@ -72,16 +90,19 @@
 
 def kernel(
     blocks_hbm, rows_hbm, cols_hbm, counts_ref, data_hbm,
-    sol_ref, search_ref, basis_ref,
+    out_hbm,
     blk, blk_t, rows_v, cols_v, pick_r, pick_c, place_r, place_c, prod,
-    tb, wb, gsend, grecv, fsend, frecv, asend, arecv, scal,
-    in_sem, blk_sem, g_ssem, g_rsem, w_ssem, w_rsem, f_ssem, f_rsem, t_ssem, t_rsem, a_ssem, a_rsem,
+    tb, wb, gsend, grecv, fsend, frecv, asend, arecv, scal, out,
+    in_sem, blk_sem, g_ssem, g_rsem, w_ssem, w_rsem, f_ssem, f_rsem, t_ssem, t_rsem, a_ssem, a_rsem, out_sem,
 ):
     r = lax.axis_index("row")
     c = lax.axis_index("col")
     x, z = r // NZ, r % NZ
     y, core = c // NC, c % NC
-    row_peers = [((x + dx) % NX) * NZ + (z + dz) % NZ for dx, dz in ROW_STEPS]
+    row_xz = [((x + dx) % NX, (z + dz) % NZ) for dx, dz in ROW_STEPS]
+    row_peers = [px * NZ + pz for px, pz in row_xz]
+    served = [((x + dx) % NX) * NZ + (z + dz) % NZ for dx, dz in SERVE_STEPS]
+    own = chunk_of(x, z)
     col_peers = [((y + dy) % NY) * NC + (core + dc) % NC for dy, dc in COL_STEPS]
 
     barrier = pltpu.get_barrier_semaphore()
@@ -97,8 +118,15 @@
     ]
     for copy in small:
         copy.start()
-    big = pltpu.make_async_copy(blocks_hbm.at[0, 0], blk, blk_sem)
-    big.start()
+    part = NB // LOADS
+    loads = [
+        pltpu.make_async_copy(
+            blocks_hbm.at[0, 0, pl.ds(i * part, part)], blk.at[pl.ds(i * part, part)], blk_sem.at[i]
+        )
+        for i in range(LOADS)
+    ]
+    for copy in loads:
+        copy.start()
     for copy in small:
         copy.wait()
 
@@ -116,39 +144,38 @@
     hot_c = one_hot(cols_v)
     pick_c[...] = hot_c.T.astype(BF16)
     place_c[...] = jnp.where(live, hot_c, 0.0).astype(BF16)
-    big.wait()
-
-    def adjoint_part(it):
+
+    def adjoint_part(it, loads=()):
         vec = tb[it]
-        block_products(blk, pick_rows(pick_r[...], vec), prod)
+        block_products(blk, pick_rows(pick_r[...], vec), prod, loads)
         part = scatter_rows(place_c[...], prod[...])
-        gsend[:, :RCH, :] = part.reshape(N_ROW, RCH, B)
-        gsend[:, RCH:, :] = jnp.broadcast_to(lane_squares(vec).reshape(1, 1, B), (N_ROW, 1, B))
+        gsend[:, :RCH, :] = part.reshape(OWN, RCH, B)
+        gsend[:, RCH:, :] = jnp.broadcast_to(lane_squares(vec).reshape(1, 1, B), (OWN, 1, B))
 
     def start_adjoint_send(it):
-        for j, p in enumerate(row_peers):
+        for p, (px, pz) in zip(row_peers, row_xz):
             pltpu.make_async_remote_copy(
-                gsend.at[p], grecv.at[it, j], g_ssem, g_rsem.at[it], device_id=(p, c), device_id_type=MESH
+                gsend.at[chunk_of(px, pz)], grecv.at[it, r], g_ssem, g_rsem.at[it], device_id=(p, c), device_id_type=MESH
             ).start()
+        grecv[it, r] = gsend[own]
 
     def finish_adjoint(it, first):
         got = grecv.at[it, pl.ds(0, N_ROW - 1)]
         pltpu.make_async_copy(got, got, g_rsem.at[it]).wait()
-        total = jnp.sum(grecv[it, : N_ROW - 1], axis=0) + gsend[r]
+        total = jnp.sum(grecv[it], axis=0)
         beta = norm_of(total[RCH:])
         chunk = total[:RCH] / beta
         if not first:
             alpha = scal[it - 1, 0:1, 0:1]
-            chunk = chunk - beta * (wb[it - 1, r] / alpha)
-        wb[it, r] = chunk
+            chunk = chunk - beta * (wb[it - 1, own] / alpha)
+        wb[it, own] = chunk
         scal[it, 1:2, :] = jnp.broadcast_to(beta, (1, B))
-        for p in row_peers:
+        for p in served:
             pltpu.make_async_remote_copy(
-                wb.at[it, r], wb.at[it, r], w_ssem, w_rsem.at[it], device_id=(p, c), device_id_type=MESH
+                wb.at[it, own], wb.at[it, own], w_ssem, w_rsem.at[it], device_id=(p, c), device_id_type=MESH
             ).start()
-        sent = gsend.at[pl.ds(0, N_ROW - 1)]
-        pltpu.make_async_copy(sent, sent, g_ssem).wait()
-        landed = wb.at[it, pl.ds(0, N_ROW - 1)]
+        pltpu.make_async_copy(got, got, g_ssem).wait()
+        landed = wb.at[it, pl.ds(0, OWN - 1)]
         pltpu.make_async_copy(landed, landed, w_rsem.at[it]).wait()
         pltpu.make_async_copy(landed, landed, w_ssem).wait()
 
@@ -158,13 +185,14 @@
         part = scatter_rows(place_r[...], prod[...])
         fsend[:, :CCH, :] = part.reshape(N_COL, CCH, B)
         fsend[:, CCH:, :] = jnp.broadcast_to(lane_squares(vec).reshape(1, 1, B), (N_COL, 1, B))
-        for j, p in enumerate(col_peers):
+        for p in col_peers:
             pltpu.make_async_remote_copy(
-                fsend.at[p], frecv.at[it, j], f_ssem, f_rsem.at[it], device_id=(r, p), device_id_type=MESH
+                fsend.at[p], frecv.at[it, c], f_ssem, f_rsem.at[it], device_id=(r, p), device_id_type=MESH
             ).start()
+        frecv[it, c] = fsend[c]
         got = frecv.at[it, pl.ds(0, N_COL - 1)]
         pltpu.make_async_copy(got, got, f_rsem.at[it]).wait()
-        total = jnp.sum(frecv[it, : N_COL - 1], axis=0) + fsend[c]
+        total = jnp.sum(frecv[it], axis=0)
         alpha = norm_of(total[CCH:])
         beta = scal[it, 1:2, 0:1]
         mine = pl.ds(pl.multiple_of(c * CCH, CCH), CCH)
@@ -182,7 +210,7 @@
         pltpu.make_async_copy(landed, landed, t_rsem.at[it]).wait()
         pltpu.make_async_copy(landed, landed, t_ssem).wait()
 
-    adjoint_part(0)
+    adjoint_part(0, loads)
     pl.semaphore_wait(barrier, N_ROW + N_COL - 2)
     start_adjoint_send(0)
 
@@ -203,14 +231,17 @@
     lax.fori_loop(0, ITERS, step, 0)
 
     asend[...] = lane_squares(wb[ITERS].reshape(NB, B))
-    for j, p in enumerate(col_peers):
+    for p in col_peers:
         pltpu.make_async_remote_copy(
-            asend, arecv.at[j], a_ssem, a_rsem, device_id=(r, p), device_id_type=MESH
+            asend, arecv.at[c], a_ssem, a_rsem, device_id=(r, p), device_id_type=MESH
         ).start()
+    arecv[c] = asend[...]
 
     alphas = [scal[i, 0:1, 0:1] for i in range(ITERS)]
     betas = [scal[i, 1:2, 0:1] for i in range(ITERS + 1)]
-    basis_ref[...] = tb[ITERS] / betas[ITERS]
+    stores = [pltpu.make_async_copy(out.at[i], out_hbm.at[i], out_sem.at[i]) for i in range(3)]
+    out[2] = tb[ITERS] / betas[ITERS]
+    stores[2].start()
     search = wb[0].reshape(NB, B) / alphas[0]
     answer = jnp.zeros((NB, B), F32)
     phibar, rhobar = betas[0], alphas[0]
@@ -225,23 +256,27 @@
             theta = sine * alphas[i + 1]
             rhobar = -cosine * alphas[i + 1]
             search = wb[i + 1].reshape(NB, B) / alphas[i + 1] - (theta / rho) * search
-    sol_ref[...] = answer
-    pltpu.make_async_copy(arecv, arecv, a_rsem).wait()
-    pltpu.make_async_copy(arecv, arecv, a_ssem).wait()
-    squares = jnp.sum(arecv[...], axis=0) + asend[...]
+    out[0] = answer
+    stores[0].start()
+    others = arecv.at[pl.ds(0, N_COL - 1)]
+    pltpu.make_async_copy(others, others, a_rsem).wait()
+    pltpu.make_async_copy(others, others, a_ssem).wait()
+    squares = jnp.sum(arecv[...], axis=0)
     alpha = norm_of(squares)
-    search_ref[...] = wb[ITERS].reshape(NB, B) / alpha - (sine * alpha / rho) * search
+    out[1] = wb[ITERS].reshape(NB, B) / alpha - (sine * alpha / rho) * search
+    stores[1].start()
+    for copy in stores:
+        copy.wait()
 
 
 def per_device(blocks, block_rows, block_cols, counts, data):
     vec = jax.ShapeDtypeStruct((NB, B), F32)
     hbm = pl.BlockSpec(memory_space=pl.ANY)
-    vmem = pl.BlockSpec(memory_space=pltpu.VMEM)
-    sol, search, basis = pl.pallas_call(
+    out = pl.pallas_call(
         kernel,
-        out_shape=(vec, vec, vec),
+        out_shape=jax.ShapeDtypeStruct((3, NB, B), F32),
         in_specs=[hbm, hbm, hbm, pl.BlockSpec(memory_space=pltpu.SMEM), hbm],
-        out_specs=(vmem, vmem, vmem),
+        out_specs=hbm,
         scratch_shapes=[
             pltpu.VMEM((NB, B, B), BF16),
             pltpu.VMEM((NB, B, B), BF16),
@@ -253,16 +288,17 @@
             pltpu.VMEM((NB, NB), BF16),
             pltpu.VMEM((NB, B), F32),
             pltpu.VMEM((ITERS + 1, NB, B), F32),
-            pltpu.VMEM((ITERS + 1, N_ROW, RCH, B), F32),
-            pltpu.VMEM((N_ROW, RCH + 1, B), F32),
+            pltpu.VMEM((ITERS + 1, OWN, RCH, B), F32),
+            pltpu.VMEM((OWN, RCH + 1, B), F32),
             pltpu.VMEM((ITERS + 1, N_ROW, RCH + 1, B), F32),
             pltpu.VMEM((N_COL, CCH + 1, B), F32),
             pltpu.VMEM((ITERS, N_COL, CCH + 1, B), F32),
             pltpu.VMEM((1, B), F32),
-            pltpu.VMEM((N_COL - 1, 1, B), F32),
+            pltpu.VMEM((N_COL, 1, B), F32),
             pltpu.VMEM((ITERS + 1, 8, B), F32),
+            pltpu.VMEM((3, NB, B), F32),
             pltpu.SemaphoreType.DMA((3,)),
-            pltpu.SemaphoreType.DMA,
+            pltpu.SemaphoreType.DMA((LOADS,)),
             pltpu.SemaphoreType.DMA,
             pltpu.SemaphoreType.DMA((ITERS + 1,)),
             pltpu.SemaphoreType.DMA,
@@ -273,13 +309,14 @@
             pltpu.SemaphoreType.DMA((ITERS,)),
             pltpu.SemaphoreType.DMA,
             pltpu.SemaphoreType.DMA,
+            pltpu.SemaphoreType.DMA((3,)),
         ],
         compiler_params=pltpu.CompilerParams(
-            collective_id=0, has_side_effects=True, vmem_limit_bytes=48 * 1024 * 1024
+            collective_id=0, has_side_effects=True, vmem_limit_bytes=56 * 1024 * 1024
         ),
         name="lsqr",
     )(blocks, block_rows[0], block_cols[0], counts, data.reshape(NB, B))
-    return sol.reshape(-1), search.reshape(-1), basis.reshape(-1)
+    return out[0].reshape(-1), out[1].reshape(-1), out[2].reshape(-1)
 
 
 def solution(mesh):

time: 104 us -> 109 us (1.048)
  Pallas kernels: 98.7 us -> 105 us
  local copies, waits for them, and re-layouts: 4.25 us -> 1.78 us
    pallas_call x1, Pallas kernels: 98.7 us -> 105 us  [per_device(): pl.pallas_call(kernel, out_shape=jax.ShapeDtypeStruct((3, NB, B), F32), i...]
    unnamed x9 -> x0, local copies, waits for them, and re-layouts: 4.25 us -> none
    another operation x0 -> x1, local copies, waits for them, and re-layouts: none -> 1.78 us  [per_device(): return (out[0].reshape(-1), out[1].reshape(-1), out[2].reshape(-1))]
where the time goes in v2:
time: 109 us; the launch traced here: 108 us
  Pallas kernels  105 us (96%)
  local copies, waits for them, and re-layouts  1.78 us (2%)
  between operations  1.29 us (1%)
    pallas_call x1, Pallas kernels, per_device(): pl.pallas_call(kernel, out_shape=jax.ShapeDtypeStruct((3, NB, B), F32), i...  105 us

profile of v2, /device:TPU:1, one launch (start us, length us, event | category | flops | bytes accessed | tf_op | source)
XLA Modules:
  0.0 108.4 jit_solution(16805952097201334947)
XLA Ops:
  1.3 105.3 %lsqr.1 = f32[3,256,128]{2,1,0:T(8,128)} custom-call(bf16[1,1,256,128,128]{4,3,2,1,0:T(8,128)(2,1)} %blocks_hbm.1, s32[1,256]{1,0:T(1,128)} %bitcast.10, s32[1,256]{1,0:T(1,128)} %bitcast.11, s32[1,1]{1,0:T(1,128)S(6)} %copy.8.counts_ref, f32[256,128]{1,0:T(8,128)} %bitcast.9), custom_call_target="tpu_custom_call" | custom-call | tf_op jit(solution)/shard_map/lsqr/pallas_call | solution.py:275
  106.6 1.8 %slice_bitcast_fusion = (f32[32768]{0:T(1024)}, f32[32768]{0:T(1024)}, f32[32768]{0:T(1024)}) fusion(f32[3,256,128]{2,1,0:T(8,128)} %lsqr.1), kind=kLoop, calls=%fused_computation | loop fusion | bytes 786432 | tf_op jit(solution)/shard_map/reshape;squeeze | solution.py:319

commit v3 on v2

--- a/solution.py
+++ b/solution.py
@@ -15,10 +15,9 @@
 NX, NZ, NY, NC = 4, 8, 4, 2
 N_ROW = NX * NZ
 N_COL = NY * NC
-OWN = N_ROW // 2
-RCH = NB // OWN
+RCH = NB // N_ROW
 LOADS = 4
-CCH = NB // N_COL
+HALF = NB // NC
 GROUP = 16
 
 
@@ -31,23 +30,10 @@
     key=lambda s: -(ring(s[0], NX) + ring(s[1], NZ)),
 )
 
-
-def nearer(step):
-    other = ((step[0] + NX // 2) % NX, (step[1] + NZ // 2) % NZ)
-    mine = (ring(step[0], NX) + ring(step[1], NZ), step)
-    return mine < (ring(other[0], NX) + ring(other[1], NZ), other)
-
-
-SERVE_STEPS = [s for s in ROW_STEPS if nearer(s)]
 COL_STEPS = sorted(
     ((dy, dc) for dy in range(NY) for dc in range(NC) if dy or dc),
     key=lambda s: -(2 * ring(s[0], NY) + s[1]),
 )
-
-
-def chunk_of(x, z):
-    upper = x // (NX // 2)
-    return (x % (NX // 2)) * NZ + (z + upper * (NZ // 2)) % NZ
 
 
 def block_products(blocks_ref, picks, out_ref, loads=()):
@@ -92,17 +78,16 @@
     blocks_hbm, rows_hbm, cols_hbm, counts_ref, data_hbm,
     out_hbm,
     blk, blk_t, rows_v, cols_v, pick_r, pick_c, place_r, place_c, prod,
-    tb, wb, gsend, grecv, fsend, frecv, asend, arecv, scal, out,
-    in_sem, blk_sem, g_ssem, g_rsem, w_ssem, w_rsem, f_ssem, f_rsem, t_ssem, t_rsem, a_ssem, a_rsem, out_sem,
+    tb, wb, gsend, grecv, fsend, frecv, psend, precv, asend, arecv, scal, out,
+    in_sem, blk_sem, g_ssem, g_rsem, w_ssem, w_rsem, f_ssem, f_rsem, p_ssem, p_rsem, t_ssem, t_rsem, a_ssem, a_rsem, out_sem,
 ):
     r = lax.axis_index("row")
     c = lax.axis_index("col")
     x, z = r // NZ, r % NZ
     y, core = c // NC, c % NC
-    row_xz = [((x + dx) % NX, (z + dz) % NZ) for dx, dz in ROW_STEPS]
-    row_peers = [px * NZ + pz for px, pz in row_xz]
-    served = [((x + dx) % NX) * NZ + (z + dz) % NZ for dx, dz in SERVE_STEPS]
-    own = chunk_of(x, z)
+    row_peers = [((x + dx) % NX) * NZ + (z + dz) % NZ for dx, dz in ROW_STEPS]
+    twin = y * NC + 1 - core
+    y_peers = [((y + dy) % NY) * NC + core for dy in (2, 1, 3)]
     col_peers = [((y + dy) % NY) * NC + (core + dc) % NC for dy, dc in COL_STEPS]
 
     barrier = pltpu.get_barrier_semaphore()
@@ -149,15 +134,15 @@
         vec = tb[it]
         block_products(blk, pick_rows(pick_r[...], vec), prod, loads)
         part = scatter_rows(place_c[...], prod[...])
-        gsend[:, :RCH, :] = part.reshape(OWN, RCH, B)
-        gsend[:, RCH:, :] = jnp.broadcast_to(lane_squares(vec).reshape(1, 1, B), (OWN, 1, B))
+        gsend[:, :RCH, :] = part.reshape(N_ROW, RCH, B)
+        gsend[:, RCH:, :] = jnp.broadcast_to(lane_squares(vec).reshape(1, 1, B), (N_ROW, 1, B))
 
     def start_adjoint_send(it):
-        for p, (px, pz) in zip(row_peers, row_xz):
+        for p in row_peers:
             pltpu.make_async_remote_copy(
-                gsend.at[chunk_of(px, pz)], grecv.at[it, r], g_ssem, g_rsem.at[it], device_id=(p, c), device_id_type=MESH
+                gsend.at[p], grecv.at[it, r], g_ssem, g_rsem.at[it], device_id=(p, c), device_id_type=MESH
             ).start()
-        grecv[it, r] = gsend[own]
+        grecv[it, r] = gsend[r]
 
     def finish_adjoint(it, first):
         got = grecv.at[it, pl.ds(0, N_ROW - 1)]
@@ -167,15 +152,15 @@
         chunk = total[:RCH] / beta
         if not first:
             alpha = scal[it - 1, 0:1, 0:1]
-            chunk = chunk - beta * (wb[it - 1, own] / alpha)
-        wb[it, own] = chunk
+            chunk = chunk - beta * (wb[it - 1, r] / alpha)
+        wb[it, r] = chunk
         scal[it, 1:2, :] = jnp.broadcast_to(beta, (1, B))
-        for p in served:
+        for p in row_peers:
             pltpu.make_async_remote_copy(
-                wb.at[it, own], wb.at[it, own], w_ssem, w_rsem.at[it], device_id=(p, c), device_id_type=MESH
+                wb.at[it, r], wb.at[it, r], w_ssem, w_rsem.at[it], device_id=(p, c), device_id_type=MESH
             ).start()
         pltpu.make_async_copy(got, got, g_ssem).wait()
-        landed = wb.at[it, pl.ds(0, OWN - 1)]
+        landed = wb.at[it, pl.ds(0, N_ROW - 1)]
         pltpu.make_async_copy(landed, landed, w_rsem.at[it]).wait()
         pltpu.make_async_copy(landed, landed, w_ssem).wait()
 
@@ -183,32 +168,35 @@
         vec = wb[it].reshape(NB, B)
         block_products(blk_t, pick_rows(pick_c[...], vec), prod)
         part = scatter_rows(place_r[...], prod[...])
-        fsend[:, :CCH, :] = part.reshape(N_COL, CCH, B)
-        fsend[:, CCH:, :] = jnp.broadcast_to(lane_squares(vec).reshape(1, 1, B), (N_COL, 1, B))
-        for p in col_peers:
+        fsend[:, :HALF, :] = part.reshape(NC, HALF, B)
+        fsend[:, HALF:, :] = jnp.broadcast_to(lane_squares(vec).reshape(1, 1, B), (NC, 1, B))
+        pair = pltpu.make_async_remote_copy(
+            fsend.at[1 - core], frecv.at[it], f_ssem, f_rsem.at[it], device_id=(r, twin), device_id_type=MESH
+        )
+        pair.start()
+        pair.wait()
+        psend[...] = fsend[core] + frecv[it]
+        for p in y_peers:
             pltpu.make_async_remote_copy(
-                fsend.at[p], frecv.at[it, c], f_ssem, f_rsem.at[it], device_id=(r, p), device_id_type=MESH
+                psend, precv.at[it, y], p_ssem, p_rsem.at[it], device_id=(r, p), device_id_type=MESH
             ).start()
-        frecv[it, c] = fsend[c]
-        got = frecv.at[it, pl.ds(0, N_COL - 1)]
-        pltpu.make_async_copy(got, got, f_rsem.at[it]).wait()
-        total = jnp.sum(frecv[it], axis=0)
-        alpha = norm_of(total[CCH:])
+        precv[it, y] = psend[...]
         beta = scal[it, 1:2, 0:1]
-        mine = pl.ds(pl.multiple_of(c * CCH, CCH), CCH)
-        tb[it + 1, mine] = total[:CCH] / alpha - alpha * (tb[it, mine] / beta)
+        mine = pl.ds(pl.multiple_of(core * HALF, HALF), HALF)
+        unit = tb[it, mine] / beta
+        got = precv.at[it, pl.ds(0, NY - 1)]
+        pltpu.make_async_copy(got, got, p_rsem.at[it]).wait()
+        total = jnp.sum(precv[it], axis=0)
+        alpha = norm_of(total[HALF:])
+        tb[it + 1, mine] = total[:HALF] / alpha - alpha * unit
+        done = pltpu.make_async_remote_copy(
+            tb.at[it + 1, mine], tb.at[it + 1, mine], t_ssem, t_rsem.at[it],
+            device_id=(r, twin), device_id_type=MESH,
+        )
+        done.start()
         scal[it, 0:1, :] = jnp.broadcast_to(alpha, (1, B))
-        for p in col_peers:
-            pltpu.make_async_remote_copy(
-                tb.at[it + 1, mine], tb.at[it + 1, mine], t_ssem, t_rsem.at[it],
-                device_id=(r, p), device_id_type=MESH,
-            ).start()
-        pltpu.make_async_copy(
-            fsend.at[pl.ds(0, N_COL - 1)], fsend.at[pl.ds(0, N_COL - 1)], f_ssem
-        ).wait()
-        landed = tb.at[it + 1, pl.ds(0, NB - CCH)]
-        pltpu.make_async_copy(landed, landed, t_rsem.at[it]).wait()
-        pltpu.make_async_copy(landed, landed, t_ssem).wait()
+        pltpu.make_async_copy(got, got, p_ssem).wait()
+        done.wait()
 
     adjoint_part(0, loads)
     pl.semaphore_wait(barrier, N_ROW + N_COL - 2)
@@ -288,11 +276,13 @@
             pltpu.VMEM((NB, NB), BF16),
             pltpu.VMEM((NB, B), F32),
             pltpu.VMEM((ITERS + 1, NB, B), F32),
-            pltpu.VMEM((ITERS + 1, OWN, RCH, B), F32),
-            pltpu.VMEM((OWN, RCH + 1, B), F32),
+            pltpu.VMEM((ITERS + 1, N_ROW, RCH, B), F32),
+            pltpu.VMEM((N_ROW, RCH + 1, B), F32),
             pltpu.VMEM((ITERS + 1, N_ROW, RCH + 1, B), F32),
-            pltpu.VMEM((N_COL, CCH + 1, B), F32),
-            pltpu.VMEM((ITERS, N_COL, CCH + 1, B), F32),
+            pltpu.VMEM((NC, HALF + 1, B), F32),
+            pltpu.VMEM((ITERS, HALF + 1, B), F32),
+            pltpu.VMEM((HALF + 1, B), F32),
+            pltpu.VMEM((ITERS, NY, HALF + 1, B), F32),
             pltpu.VMEM((1, B), F32),
             pltpu.VMEM((N_COL, 1, B), F32),
             pltpu.VMEM((ITERS + 1, 8, B), F32),
@@ -303,6 +293,8 @@
             pltpu.SemaphoreType.DMA((ITERS + 1,)),
             pltpu.SemaphoreType.DMA,
             pltpu.SemaphoreType.DMA((ITERS + 1,)),
+            pltpu.SemaphoreType.DMA,
+            pltpu.SemaphoreType.DMA((ITERS,)),
             pltpu.SemaphoreType.DMA,
             pltpu.SemaphoreType.DMA((ITERS,)),
             pltpu.SemaphoreType.DMA,

time: 109 us -> 103 us (0.945)
  Pallas kernels: 105 us -> 99.8 us
    pallas_call x1, Pallas kernels: 105 us -> 99.8 us  [per_device(): pl.pallas_call(kernel, out_shape=jax.ShapeDtypeStruct((3, NB, B), F32), i...]
where the time goes in v3:
time: 103 us
  Pallas kernels  99.8 us (97%)
  local copies, waits for them, and re-layouts  1.78 us (2%)
  between operations  1.29 us (1%)
    pallas_call x1, Pallas kernels, per_device(): pl.pallas_call(kernel, out_shape=jax.ShapeDtypeStruct((3, NB, B), F32), i...  99.8 us

profile of v3, /device:TPU:1, one launch (start us, length us, event | category | flops | bytes accessed | tf_op | source)
XLA Modules:
  0.0 102.8 jit_solution(4737942206773280608)
XLA Ops:
  1.3 99.8 %lsqr.1 = f32[3,256,128]{2,1,0:T(8,128)} custom-call(bf16[1,1,256,128,128]{4,3,2,1,0:T(8,128)(2,1)} %blocks_hbm.1, s32[1,256]{1,0:T(1,128)} %bitcast.10, s32[1,256]{1,0:T(1,128)} %bitcast.11, s32[1,1]{1,0:T(1,128)S(6)} %copy.8.counts_ref, f32[256,128]{1,0:T(8,128)} %bitcast.9), custom_call_target="tpu_custom_call" | custom-call | tf_op jit(solution)/shard_map/lsqr/pallas_call | solution.py:263
  101.0 1.8 %slice_bitcast_fusion = (f32[32768]{0:T(1024)}, f32[32768]{0:T(1024)}, f32[32768]{0:T(1024)}) fusion(f32[3,256,128]{2,1,0:T(8,128)} %lsqr.1), kind=kLoop, calls=%fused_computation | loop fusion | bytes 786432 | tf_op jit(solution)/shard_map/reshape;squeeze | solution.py:311

commit v4 on v3

--- a/solution.py
+++ b/solution.py
@@ -16,7 +16,7 @@
 N_ROW = NX * NZ
 N_COL = NY * NC
 RCH = NB // N_ROW
-LOADS = 4
+LOADS = 8
 HALF = NB // NC
 GROUP = 16
 
@@ -90,12 +90,6 @@
     y_peers = [((y + dy) % NY) * NC + core for dy in (2, 1, 3)]
     col_peers = [((y + dy) % NY) * NC + (core + dc) % NC for dy, dc in COL_STEPS]
 
-    barrier = pltpu.get_barrier_semaphore()
-    for p in row_peers:
-        pl.semaphore_signal(barrier, inc=1, device_id=(p, c), device_id_type=MESH)
-    for p in col_peers:
-        pl.semaphore_signal(barrier, inc=1, device_id=(r, p), device_id_type=MESH)
-
     small = [
         pltpu.make_async_copy(rows_hbm, rows_v, in_sem.at[0]),
         pltpu.make_async_copy(cols_hbm, cols_v, in_sem.at[1]),
@@ -112,6 +106,13 @@
     ]
     for copy in loads:
         copy.start()
+
+    barrier = pltpu.get_barrier_semaphore()
+    for p in row_peers:
+        pl.semaphore_signal(barrier, inc=1, device_id=(p, c), device_id_type=MESH)
+    for p in col_peers:
+        pl.semaphore_signal(barrier, inc=1, device_id=(r, p), device_id_type=MESH)
+
     for copy in small:
         copy.wait()
 
@@ -123,12 +124,8 @@
     def one_hot(index_ref):
         return (sub == index_ref[...]).astype(F32)
 
-    hot_r = one_hot(rows_v)
-    pick_r[...] = hot_r.T.astype(BF16)
-    place_r[...] = jnp.where(live, hot_r, 0.0).astype(BF16)
-    hot_c = one_hot(cols_v)
-    pick_c[...] = hot_c.T.astype(BF16)
-    place_c[...] = jnp.where(live, hot_c, 0.0).astype(BF16)
+    pick_r[...] = one_hot(rows_v).T.astype(BF16)
+    place_c[...] = jnp.where(live, one_hot(cols_v), 0.0).astype(BF16)
 
     def adjoint_part(it, loads=()):
         vec = tb[it]
@@ -167,22 +164,25 @@
     def forward(it):
         vec = wb[it].reshape(NB, B)
         block_products(blk_t, pick_rows(pick_c[...], vec), prod)
-        part = scatter_rows(place_r[...], prod[...])
-        fsend[:, :HALF, :] = part.reshape(NC, HALF, B)
-        fsend[:, HALF:, :] = jnp.broadcast_to(lane_squares(vec).reshape(1, 1, B), (NC, 1, B))
+        squares = lane_squares(vec)
+        theirs = pl.ds(pl.multiple_of((1 - core) * HALF, HALF), HALF)
+        mine = pl.ds(pl.multiple_of(core * HALF, HALF), HALF)
+        fsend[:HALF, :] = scatter_rows(place_r[theirs, :], prod[...])
+        fsend[HALF:, :] = squares
         pair = pltpu.make_async_remote_copy(
-            fsend.at[1 - core], frecv.at[it], f_ssem, f_rsem.at[it], device_id=(r, twin), device_id_type=MESH
+            fsend, frecv.at[it], f_ssem, f_rsem.at[it], device_id=(r, twin), device_id_type=MESH
         )
         pair.start()
+        psend[:HALF, :] = scatter_rows(place_r[mine, :], prod[...])
+        psend[HALF:, :] = squares
         pair.wait()
-        psend[...] = fsend[core] + frecv[it]
+        psend[...] = psend[...] + frecv[it]
         for p in y_peers:
             pltpu.make_async_remote_copy(
                 psend, precv.at[it, y], p_ssem, p_rsem.at[it], device_id=(r, p), device_id_type=MESH
             ).start()
         precv[it, y] = psend[...]
         beta = scal[it, 1:2, 0:1]
-        mine = pl.ds(pl.multiple_of(core * HALF, HALF), HALF)
         unit = tb[it, mine] / beta
         got = precv.at[it, pl.ds(0, NY - 1)]
         pltpu.make_async_copy(got, got, p_rsem.at[it]).wait()
@@ -206,7 +206,9 @@
         blk_t[k] = blk[k].T
         return carry
 
-    lax.fori_loop(0, NB, transpose_block, 0, unroll=8)
+    pick_c[...] = one_hot(cols_v).T.astype(BF16)
+    place_r[...] = jnp.where(live, one_hot(rows_v), 0.0).astype(BF16)
+    lax.fori_loop(0, NB, transpose_block, 0, unroll=16)
     finish_adjoint(0, True)
 
     def step(it, carry):
@@ -257,6 +259,17 @@
         copy.wait()
 
 
+def hand_out(out_hbm, sol_hbm, search_hbm, basis_hbm, sem):
+    copies = [
+        pltpu.make_async_copy(out_hbm.at[i], ref, sem.at[i])
+        for i, ref in enumerate((sol_hbm, search_hbm, basis_hbm))
+    ]
+    for copy in copies:
+        copy.start()
+    for copy in copies:
+        copy.wait()
+
+
 def per_device(blocks, block_rows, block_cols, counts, data):
     vec = jax.ShapeDtypeStruct((NB, B), F32)
     hbm = pl.BlockSpec(memory_space=pl.ANY)
@@ -279,7 +292,7 @@
             pltpu.VMEM((ITERS + 1, N_ROW, RCH, B), F32),
             pltpu.VMEM((N_ROW, RCH + 1, B), F32),
             pltpu.VMEM((ITERS + 1, N_ROW, RCH + 1, B), F32),
-            pltpu.VMEM((NC, HALF + 1, B), F32),
+            pltpu.VMEM((HALF + 1, B), F32),
             pltpu.VMEM((ITERS, HALF + 1, B), F32),
             pltpu.VMEM((HALF + 1, B), F32),
             pltpu.VMEM((ITERS, NY, HALF + 1, B), F32),
@@ -308,7 +321,16 @@
         ),
         name="lsqr",
     )(blocks, block_rows[0], block_cols[0], counts, data.reshape(NB, B))
-    return out[0].reshape(-1), out[1].reshape(-1), out[2].reshape(-1)
+    results = pl.pallas_call(
+        hand_out,
+        out_shape=(vec, vec, vec),
+        in_specs=[hbm],
+        out_specs=(hbm, hbm, hbm),
+        scratch_shapes=[pltpu.SemaphoreType.DMA((3,))],
+        compiler_params=pltpu.CompilerParams(vmem_limit_bytes=56 * 1024 * 1024),
+        name="hand_out",
+    )(out)
+    return tuple(a.reshape(-1) for a in results)
 
 
 def solution(mesh):

time: 103 us -> 114 us (1.11)
  Pallas kernels: 99.8 us -> 113 us
  local copies, waits for them, and re-layouts: 1.78 us -> 0 us
    pallas_call x0 -> x1, Pallas kernels: none -> 13 us  [per_device(): pl.pallas_call(hand_out, out_shape=(vec, vec, vec), in_specs=[hbm], out_s...]
    another operation x1 -> x0, local copies, waits for them, and re-layouts: 1.78 us -> none  [per_device(): return (out[0].reshape(-1), out[1].reshape(-1), out[2].reshape(-1))]
where the time goes in v4:
time: 114 us
  Pallas kernels  113 us (99%)
  between operations  1.29 us (1%)
    pallas_call x1, Pallas kernels, per_device(): pl.pallas_call(kernel, out_shape=jax.ShapeDtypeStruct((3, NB, B), F32), i...  100 us
    pallas_call x1, Pallas kernels, per_device(): pl.pallas_call(hand_out, out_shape=(vec, vec, vec), in_specs=[hbm], out_s...  13 us

profile of v4, /device:TPU:1, one launch (start us, length us, event | category | flops | bytes accessed | tf_op | source)
XLA Modules:
  0.0 114.3 jit_solution(3410310518497216209)
XLA Ops:
  1.3 100.0 %lsqr.1.out_hbm = f32[3,256,128]{2,1,0:T(8,128)} custom-call(bf16[1,1,256,128,128]{4,3,2,1,0:T(8,128)(2,1)} %blocks_hbm.1, s32[1,256]{1,0:T(1,128)} %bitcast.7, s32[1,256]{1,0:T(1,128)} %bitcast.8, s32[1,1]{1,0:T(1,128)S(6)} %copy.8.counts_ref, f32[256,128]{1,0:T(8,128)} %bitcast.6), custom_call_target="tpu_custom_call" | custom-call | tf_op jit(solution)/shard_map/lsqr/pallas_call | solution.py:276
  101.3 13.0 %hand_out.1 = (f32[256,128]{1,0:T(8,128)}, f32[256,128]{1,0:T(8,128)}, f32[256,128]{1,0:T(8,128)}) custom-call(f32[3,256,128]{2,1,0:T(8,128)} %lsqr.1.out_hbm), custom_call_target="tpu_custom_call" | custom-call | tf_op jit(solution)/shard_map/hand_out/pallas_call | solution.py:324

commit v5 on v3

--- a/solution.py
+++ b/solution.py
@@ -76,10 +76,10 @@
 
 def kernel(
     blocks_hbm, rows_hbm, cols_hbm, counts_ref, data_hbm,
-    out_hbm,
+    out,
     blk, blk_t, rows_v, cols_v, pick_r, pick_c, place_r, place_c, prod,
-    tb, wb, gsend, grecv, fsend, frecv, psend, precv, asend, arecv, scal, out,
-    in_sem, blk_sem, g_ssem, g_rsem, w_ssem, w_rsem, f_ssem, f_rsem, p_ssem, p_rsem, t_ssem, t_rsem, a_ssem, a_rsem, out_sem,
+    tb, wb, gsend, grecv, fsend, frecv, psend, precv, asend, arecv, scal,
+    in_sem, blk_sem, g_ssem, g_rsem, w_ssem, w_rsem, f_ssem, f_rsem, p_ssem, p_rsem, t_ssem, t_rsem, a_ssem, a_rsem,
 ):
     r = lax.axis_index("row")
     c = lax.axis_index("col")
@@ -145,14 +145,14 @@
         grecv[it, r] = gsend[r]
 
     def finish_adjoint(it, first):
+        before = None if first else wb[it - 1, r] / scal[it - 1, 0:1, 0:1]
         got = grecv.at[it, pl.ds(0, N_ROW - 1)]
         pltpu.make_async_copy(got, got, g_rsem.at[it]).wait()
         total = jnp.sum(grecv[it], axis=0)
         beta = norm_of(total[RCH:])
         chunk = total[:RCH] / beta
         if not first:
-            alpha = scal[it - 1, 0:1, 0:1]
-            chunk = chunk - beta * (wb[it - 1, r] / alpha)
+            chunk = chunk - beta * before
         wb[it, r] = chunk
         scal[it, 1:2, :] = jnp.broadcast_to(beta, (1, B))
         for p in row_peers:
@@ -227,9 +227,7 @@
 
     alphas = [scal[i, 0:1, 0:1] for i in range(ITERS)]
     betas = [scal[i, 1:2, 0:1] for i in range(ITERS + 1)]
-    stores = [pltpu.make_async_copy(out.at[i], out_hbm.at[i], out_sem.at[i]) for i in range(3)]
     out[2] = tb[ITERS] / betas[ITERS]
-    stores[2].start()
     search = wb[0].reshape(NB, B) / alphas[0]
     answer = jnp.zeros((NB, B), F32)
     phibar, rhobar = betas[0], alphas[0]
@@ -245,26 +243,26 @@
             rhobar = -cosine * alphas[i + 1]
             search = wb[i + 1].reshape(NB, B) / alphas[i + 1] - (theta / rho) * search
     out[0] = answer
-    stores[0].start()
     others = arecv.at[pl.ds(0, N_COL - 1)]
     pltpu.make_async_copy(others, others, a_rsem).wait()
     pltpu.make_async_copy(others, others, a_ssem).wait()
     squares = jnp.sum(arecv[...], axis=0)
     alpha = norm_of(squares)
     out[1] = wb[ITERS].reshape(NB, B) / alpha - (sine * alpha / rho) * search
-    stores[1].start()
-    for copy in stores:
-        copy.wait()
 
 
 def per_device(blocks, block_rows, block_cols, counts, data):
     vec = jax.ShapeDtypeStruct((NB, B), F32)
     hbm = pl.BlockSpec(memory_space=pl.ANY)
+
+    def in_hbm(a):
+        return pltpu.with_memory_space_constraint(a, pltpu.HBM)
+
     out = pl.pallas_call(
         kernel,
         out_shape=jax.ShapeDtypeStruct((3, NB, B), F32),
         in_specs=[hbm, hbm, hbm, pl.BlockSpec(memory_space=pltpu.SMEM), hbm],
-        out_specs=hbm,
+        out_specs=pl.BlockSpec(memory_space=pltpu.VMEM),
         scratch_shapes=[
             pltpu.VMEM((NB, B, B), BF16),
             pltpu.VMEM((NB, B, B), BF16),
@@ -286,7 +284,6 @@
             pltpu.VMEM((1, B), F32),
             pltpu.VMEM((N_COL, 1, B), F32),
             pltpu.VMEM((ITERS + 1, 8, B), F32),
-            pltpu.VMEM((3, NB, B), F32),
             pltpu.SemaphoreType.DMA((3,)),
             pltpu.SemaphoreType.DMA((LOADS,)),
             pltpu.SemaphoreType.DMA,
@@ -301,13 +298,12 @@
             pltpu.SemaphoreType.DMA((ITERS,)),
             pltpu.SemaphoreType.DMA,
             pltpu.SemaphoreType.DMA,
-            pltpu.SemaphoreType.DMA((3,)),
         ],
         compiler_params=pltpu.CompilerParams(
-            collective_id=0, has_side_effects=True, vmem_limit_bytes=56 * 1024 * 1024
+            collective_id=0, has_side_effects=True, vmem_limit_bytes=53000 * 1024
         ),
         name="lsqr",
-    )(blocks, block_rows[0], block_cols[0], counts, data.reshape(NB, B))
+    )(blocks, in_hbm(block_rows[0]), in_hbm(block_cols[0]), counts, in_hbm(data.reshape(NB, B)))
     return out[0].reshape(-1), out[1].reshape(-1), out[2].reshape(-1)
 
 

time: 103 us -> 101 us (0.981)
  local copies, waits for them, and re-layouts: 1.78 us -> 0.75 us
    another operation x1, local copies, waits for them, and re-layouts: 1.78 us -> 0.75 us  [per_device(): return (out[0].reshape(-1), out[1].reshape(-1), out[2].reshape(-1))]
where the time goes in v5:
time: 101 us
  Pallas kernels  99.1 us (98%)
  between operations  1.29 us (1%)
    pallas_call x1, Pallas kernels, per_device(): pl.pallas_call(kernel, out_shape=jax.ShapeDtypeStruct((3, NB, B), F32), i...  99.1 us

profile of v5, /device:TPU:1, one launch (start us, length us, event | category | flops | bytes accessed | tf_op | source)
XLA Modules:
  0.0 101.1 jit_solution(3088384793578857502)
XLA Ops:
  1.3 99.1 %lsqr.1 = f32[3,256,128]{2,1,0:T(8,128)S(1)} custom-call(bf16[1,1,256,128,128]{4,3,2,1,0:T(8,128)(2,1)} %blocks_hbm.1, s32[1,256]{1,0:T(1,128)} %bitcast.10, s32[1,256]{1,0:T(1,128)} %bitcast.11, s32[1,1]{1,0:T(1,128)S(6)} %copy.8.counts_ref, f32[256,128]{1,0:T(8,128)} %bitcast.9), custom_call_target="tpu_custom_call" | custom-call | tf_op jit(solution)/shard_map/lsqr/pallas_call | solution.py:261
  100.4 0.8 slice_bitcast_fusion

commit v6 on v5

--- a/solution.py
+++ b/solution.py
@@ -54,6 +54,70 @@
         out_ref[base : base + GROUP, :] = jnp.where(row < half, res[:, :B], res[:, B:])
 
 
+def swap_lanes(a):
+    return jnp.concatenate([a[:, B // 2 :], a[:, : B // 2]], axis=1)
+
+
+def left_lanes(rows):
+    return lax.broadcasted_iota(jnp.int32, (rows, B), 1) < B // 2
+
+
+def halves(vector):
+    low, high = vector[:HALF], vector[HALF:]
+    left = left_lanes(HALF)
+    return jnp.where(left, low, swap_lanes(high)), jnp.where(left, swap_lanes(low), high)
+
+
+def whole(first, second):
+    left = left_lanes(HALF)
+    return jnp.where(left, first, swap_lanes(second)), jnp.where(left, swap_lanes(first), second)
+
+
+def pick_half(pick, packed):
+    packed = packed.astype(BF16)
+    low = jnp.dot(pick[:, :HALF], packed, preferred_element_type=F32)
+    high = jnp.dot(pick[:, HALF:], packed, preferred_element_type=F32)
+    mixed = jnp.where(left_lanes(NB), low, high)
+    return mixed + swap_lanes(mixed)
+
+
+def half_adjoint_products(blocks_ref, h, picks, out_ref, add):
+    row = lax.broadcasted_iota(jnp.int32, (GROUP, B), 0)
+    side = jnp.where(left_lanes(GROUP), 0, 1)
+    half = GROUP // 2
+    rows = pl.ds(pl.multiple_of(h * (B // 2), B // 2), B // 2)
+    for g in range(NB // GROUP):
+        base = g * GROUP
+        mine = picks[base : base + GROUP]
+        lhs = jnp.concatenate(
+            [jnp.where((row & (half - 1)) == q + side, mine, 0.0).astype(BF16) for q in range(0, half, 2)], axis=1
+        )
+        left = jnp.concatenate([blocks_ref[base + q, rows] for q in range(half)], axis=0)
+        right = jnp.concatenate([blocks_ref[base + half + q, rows] for q in range(half)], axis=0)
+        res = jnp.dot(lhs, jnp.concatenate([left, right], axis=1), preferred_element_type=F32)
+        res = jnp.where(row < half, res[:, :B], res[:, B:])
+        if add:
+            res = res + out_ref[base : base + GROUP, :]
+        out_ref[base : base + GROUP, :] = res
+
+
+def half_forward_products(blk_t, h, picks, out_ref):
+    wide = 2 * GROUP
+    row = lax.broadcasted_iota(jnp.int32, (wide, B), 0)
+    keep = ((lax.broadcasted_iota(jnp.int32, (GROUP, B), 0) < 8) & left_lanes(GROUP)) | (
+        (lax.broadcasted_iota(jnp.int32, (GROUP, B), 0) >= 8) & ~left_lanes(GROUP)
+    )
+    for g in range(NB // wide):
+        base = g * wide
+        mine = picks[base : base + wide]
+        lhs = jnp.concatenate([jnp.where((row & 7) == q, mine, 0.0).astype(BF16) for q in range(8)], axis=1)
+        left = jnp.concatenate([blk_t[h, (g * 8 + q) * 2] for q in range(8)], axis=0)
+        right = jnp.concatenate([blk_t[h, (g * 8 + q) * 2 + 1] for q in range(8)], axis=0)
+        res = jnp.dot(lhs, jnp.concatenate([left, right], axis=1), preferred_element_type=F32)
+        out_ref[base : base + GROUP, :] = jnp.where(keep, res[:GROUP, :B], 0.0)
+        out_ref[base + GROUP : base + wide, :] = jnp.where(keep, res[GROUP:, B:], 0.0)
+
+
 def pick_rows(pick, vector):
     return jnp.dot(pick, vector.astype(BF16), preferred_element_type=F32)
 
@@ -78,7 +142,7 @@
     blocks_hbm, rows_hbm, cols_hbm, counts_ref, data_hbm,
     out,
     blk, blk_t, rows_v, cols_v, pick_r, pick_c, place_r, place_c, prod,
-    tb, wb, gsend, grecv, fsend, frecv, psend, precv, asend, arecv, scal,
+    data, tb, wb, gsend, grecv, fsend, frecv, psend, precv, asend, arecv, scal,
     in_sem, blk_sem, g_ssem, g_rsem, w_ssem, w_rsem, f_ssem, f_rsem, p_ssem, p_rsem, t_ssem, t_rsem, a_ssem, a_rsem,
 ):
     r = lax.axis_index("row")
@@ -99,7 +163,7 @@
     small = [
         pltpu.make_async_copy(rows_hbm, rows_v, in_sem.at[0]),
         pltpu.make_async_copy(cols_hbm, cols_v, in_sem.at[1]),
-        pltpu.make_async_copy(data_hbm, tb.at[0], in_sem.at[2]),
+        pltpu.make_async_copy(data_hbm, data, in_sem.at[2]),
     ]
     for copy in small:
         copy.start()
@@ -130,12 +194,10 @@
     pick_c[...] = hot_c.T.astype(BF16)
     place_c[...] = jnp.where(live, hot_c, 0.0).astype(BF16)
 
-    def adjoint_part(it, loads=()):
-        vec = tb[it]
-        block_products(blk, pick_rows(pick_r[...], vec), prod, loads)
+    def adjoint_place(squares):
         part = scatter_rows(place_c[...], prod[...])
         gsend[:, :RCH, :] = part.reshape(N_ROW, RCH, B)
-        gsend[:, RCH:, :] = jnp.broadcast_to(lane_squares(vec).reshape(1, 1, B), (N_ROW, 1, B))
+        gsend[:, RCH:, :] = jnp.broadcast_to(squares.reshape(1, 1, B), (N_ROW, 1, B))
 
     def start_adjoint_send(it):
         for p in row_peers:
@@ -164,54 +226,67 @@
         pltpu.make_async_copy(landed, landed, w_rsem.at[it]).wait()
         pltpu.make_async_copy(landed, landed, w_ssem).wait()
 
-    def forward(it):
+    def forward_half(h, picks):
+        half_forward_products(blk_t, h, picks, prod)
+        both = scatter_rows(place_r[...], prod[...])
+        both = both + swap_lanes(both)
+        return jnp.where(left_lanes(HALF), both[:HALF], both[HALF:])
+
+    def forward_and_adjoint(it):
         vec = wb[it].reshape(NB, B)
-        block_products(blk_t, pick_rows(pick_c[...], vec), prod)
-        part = scatter_rows(place_r[...], prod[...])
-        fsend[:, :HALF, :] = part.reshape(NC, HALF, B)
-        fsend[:, HALF:, :] = jnp.broadcast_to(lane_squares(vec).reshape(1, 1, B), (NC, 1, B))
+        picks = pick_rows(pick_c[...], vec)
+        squares = lane_squares(vec)
+        fsend[:HALF, :] = forward_half(1 - core, picks)
+        fsend[HALF:, :] = squares
         pair = pltpu.make_async_remote_copy(
-            fsend.at[1 - core], frecv.at[it], f_ssem, f_rsem.at[it], device_id=(r, twin), device_id_type=MESH
+            fsend, frecv.at[it], f_ssem, f_rsem.at[it], device_id=(r, twin), device_id_type=MESH
         )
         pair.start()
+        psend[:HALF, :] = forward_half(core, picks)
+        psend[HALF:, :] = squares
         pair.wait()
-        psend[...] = fsend[core] + frecv[it]
+        psend[...] = psend[...] + frecv[it]
         for p in y_peers:
             pltpu.make_async_remote_copy(
                 psend, precv.at[it, y], p_ssem, p_rsem.at[it], device_id=(r, p), device_id_type=MESH
             ).start()
         precv[it, y] = psend[...]
-        beta = scal[it, 1:2, 0:1]
-        mine = pl.ds(pl.multiple_of(core * HALF, HALF), HALF)
-        unit = tb[it, mine] / beta
+        unit = tb[it, core] / scal[it, 1:2, 0:1]
         got = precv.at[it, pl.ds(0, NY - 1)]
         pltpu.make_async_copy(got, got, p_rsem.at[it]).wait()
         total = jnp.sum(precv[it], axis=0)
         alpha = norm_of(total[HALF:])
-        tb[it + 1, mine] = total[:HALF] / alpha - alpha * unit
+        tb[it + 1, core] = total[:HALF] / alpha - alpha * unit
         done = pltpu.make_async_remote_copy(
-            tb.at[it + 1, mine], tb.at[it + 1, mine], t_ssem, t_rsem.at[it],
+            tb.at[it + 1, core], tb.at[it + 1, core], t_ssem, t_rsem.at[it],
             device_id=(r, twin), device_id_type=MESH,
         )
         done.start()
         scal[it, 0:1, :] = jnp.broadcast_to(alpha, (1, B))
+        half_adjoint_products(blk, core, pick_half(pick_r[...], tb[it + 1, core]), prod, False)
         pltpu.make_async_copy(got, got, p_ssem).wait()
         done.wait()
-
-    adjoint_part(0, loads)
+        half_adjoint_products(blk, 1 - core, pick_half(pick_r[...], tb[it + 1, 1 - core]), prod, True)
+        adjoint_place(lane_squares(tb[it + 1, 0]) + lane_squares(tb[it + 1, 1]))
+
+    block_products(blk, pick_rows(pick_r[...], data[...]), prod, loads)
+    adjoint_place(lane_squares(data[...]))
     pl.semaphore_wait(barrier, N_ROW + N_COL - 2)
     start_adjoint_send(0)
-
-    def transpose_block(k, carry):
-        blk_t[k] = blk[k].T
+    tb[0, 0], tb[0, 1] = halves(data[...])
+
+    def transpose_pair(n, carry):
+        first = (n // 16) * 32 + (n % 2) * 16 + (n // 2) % 8
+        for h in range(2):
+            rows = slice(h * (B // 2), (h + 1) * (B // 2))
+            blk_t[h, n] = jnp.concatenate([blk[first, rows], blk[first + 8, rows]], axis=0).T
         return carry
 
-    lax.fori_loop(0, NB, transpose_block, 0, unroll=8)
+    lax.fori_loop(0, NB // 2, transpose_pair, 0, unroll=8)
     finish_adjoint(0, True)
 
     def step(it, carry):
-        forward(it)
-        adjoint_part(it + 1)
+        forward_and_adjoint(it)
         start_adjoint_send(it + 1)
         finish_adjoint(it + 1, False)
         return carry
@@ -227,7 +302,9 @@
 
     alphas = [scal[i, 0:1, 0:1] for i in range(ITERS)]
     betas = [scal[i, 1:2, 0:1] for i in range(ITERS + 1)]
-    out[2] = tb[ITERS] / betas[ITERS]
+    top, bottom = whole(tb[ITERS, 0] / betas[ITERS], tb[ITERS, 1] / betas[ITERS])
+    out[2, :HALF] = top
+    out[2, HALF:] = bottom
     search = wb[0].reshape(NB, B) / alphas[0]
     answer = jnp.zeros((NB, B), F32)
     phibar, rhobar = betas[0], alphas[0]
@@ -265,7 +342,7 @@
         out_specs=pl.BlockSpec(memory_space=pltpu.VMEM),
         scratch_shapes=[
             pltpu.VMEM((NB, B, B), BF16),
-            pltpu.VMEM((NB, B, B), BF16),
+            pltpu.VMEM((2, NB // 2, B, B), BF16),
             pltpu.VMEM((1, NB), jnp.int32),
             pltpu.VMEM((1, NB), jnp.int32),
             pltpu.VMEM((NB, NB), BF16),
@@ -273,11 +350,12 @@
             pltpu.VMEM((NB, NB), BF16),
             pltpu.VMEM((NB, NB), BF16),
             pltpu.VMEM((NB, B), F32),
-            pltpu.VMEM((ITERS + 1, NB, B), F32),
+            pltpu.VMEM((NB, B), F32),
+            pltpu.VMEM((ITERS + 1, 2, HALF, B), F32),
             pltpu.VMEM((ITERS + 1, N_ROW, RCH, B), F32),
             pltpu.VMEM((N_ROW, RCH + 1, B), F32),
             pltpu.VMEM((ITERS + 1, N_ROW, RCH + 1, B), F32),
-            pltpu.VMEM((NC, HALF + 1, B), F32),
+            pltpu.VMEM((HALF + 1, B), F32),
             pltpu.VMEM((ITERS, HALF + 1, B), F32),
             pltpu.VMEM((HALF + 1, B), F32),
             pltpu.VMEM((ITERS, NY, HALF + 1, B), F32),

time: 101 us -> 98.5 us (0.975)
  Pallas kernels: 99.1 us -> 96.3 us
    pallas_call x1, Pallas kernels: 99.1 us -> 96.3 us  [per_device(): pl.pallas_call(kernel, out_shape=jax.ShapeDtypeStruct((3, NB, B), F32), i...]
where the time goes in v6:
time: 98.5 us; the launch traced here: 98.4 us
  Pallas kernels  96.3 us (98%)
  between operations  1.29 us (1%)
    pallas_call x1, Pallas kernels, per_device(): pl.pallas_call(kernel, out_shape=jax.ShapeDtypeStruct((3, NB, B), F32), i...  96.3 us

profile of v6, /device:TPU:1, one launch (start us, length us, event | category | flops | bytes accessed | tf_op | source)
XLA Modules:
  0.0 98.4 jit_solution(10633537473587319723)
XLA Ops:
  1.3 96.3 %lsqr.1 = f32[3,256,128]{2,1,0:T(8,128)S(1)} custom-call(bf16[1,1,256,128,128]{4,3,2,1,0:T(8,128)(2,1)} %blocks_hbm.1, s32[1,256]{1,0:T(1,128)} %bitcast.10, s32[1,256]{1,0:T(1,128)} %bitcast.11, s32[1,1]{1,0:T(1,128)S(6)} %copy.8.counts_ref, f32[256,128]{1,0:T(8,128)} %bitcast.9), custom_call_target="tpu_custom_call" | custom-call | tf_op jit(solution)/shard_map/lsqr/pallas_call | solution.py:338
  97.6 0.8 slice_bitcast_fusion

commit v7 on v6

--- a/solution.py
+++ b/solution.py
@@ -142,8 +142,8 @@
     blocks_hbm, rows_hbm, cols_hbm, counts_ref, data_hbm,
     out,
     blk, blk_t, rows_v, cols_v, pick_r, pick_c, place_r, place_c, prod,
-    data, tb, wb, gsend, grecv, fsend, frecv, psend, precv, asend, arecv, scal,
-    in_sem, blk_sem, g_ssem, g_rsem, w_ssem, w_rsem, f_ssem, f_rsem, p_ssem, p_rsem, t_ssem, t_rsem, a_ssem, a_rsem,
+    data, tb, wb, gsend, grecv, fsend, frecv, psend, precv, asend, arecv, bsend, brecv, scal,
+    in_sem, blk_sem, g_ssem, g_rsem, w_ssem, w_rsem, f_ssem, f_rsem, p_ssem, p_rsem, t_ssem, t_rsem, a_ssem, a_rsem, b_ssem, b_rsem,
 ):
     r = lax.axis_index("row")
     c = lax.axis_index("col")
@@ -206,6 +206,23 @@
             ).start()
         grecv[it, r] = gsend[r]
 
+    def start_last_norm():
+        asend[...] = lane_squares(wb[ITERS, r])
+        for p in col_peers:
+            pltpu.make_async_remote_copy(
+                asend, arecv.at[c], a_ssem, a_rsem, device_id=(r, p), device_id_type=MESH
+            ).start()
+        arecv[c] = asend[...]
+        others = arecv.at[pl.ds(0, N_COL - 1)]
+        pltpu.make_async_copy(others, others, a_rsem).wait()
+        bsend[...] = jnp.sum(arecv[...], axis=0)
+        for p in row_peers:
+            pltpu.make_async_remote_copy(
+                bsend, brecv.at[r], b_ssem, b_rsem, device_id=(p, c), device_id_type=MESH
+            ).start()
+        brecv[r] = bsend[...]
+        pltpu.make_async_copy(others, others, a_ssem).wait()
+
     def finish_adjoint(it, first):
         before = None if first else wb[it - 1, r] / scal[it - 1, 0:1, 0:1]
         got = grecv.at[it, pl.ds(0, N_ROW - 1)]
@@ -221,6 +238,8 @@
             pltpu.make_async_remote_copy(
                 wb.at[it, r], wb.at[it, r], w_ssem, w_rsem.at[it], device_id=(p, c), device_id_type=MESH
             ).start()
+        if not first:
+            pl.when(it == ITERS)(start_last_norm)
         pltpu.make_async_copy(got, got, g_ssem).wait()
         landed = wb.at[it, pl.ds(0, N_ROW - 1)]
         pltpu.make_async_copy(landed, landed, w_rsem.at[it]).wait()
@@ -293,13 +312,6 @@
 
     lax.fori_loop(0, ITERS, step, 0)
 
-    asend[...] = lane_squares(wb[ITERS].reshape(NB, B))
-    for p in col_peers:
-        pltpu.make_async_remote_copy(
-            asend, arecv.at[c], a_ssem, a_rsem, device_id=(r, p), device_id_type=MESH
-        ).start()
-    arecv[c] = asend[...]
-
     alphas = [scal[i, 0:1, 0:1] for i in range(ITERS)]
     betas = [scal[i, 1:2, 0:1] for i in range(ITERS + 1)]
     top, bottom = whole(tb[ITERS, 0] / betas[ITERS], tb[ITERS, 1] / betas[ITERS])
@@ -320,12 +332,11 @@
             rhobar = -cosine * alphas[i + 1]
             search = wb[i + 1].reshape(NB, B) / alphas[i + 1] - (theta / rho) * search
     out[0] = answer
-    others = arecv.at[pl.ds(0, N_COL - 1)]
-    pltpu.make_async_copy(others, others, a_rsem).wait()
-    pltpu.make_async_copy(others, others, a_ssem).wait()
-    squares = jnp.sum(arecv[...], axis=0)
-    alpha = norm_of(squares)
+    others = brecv.at[pl.ds(0, N_ROW - 1)]
+    pltpu.make_async_copy(others, others, b_rsem).wait()
+    alpha = norm_of(jnp.sum(brecv[...], axis=0))
     out[1] = wb[ITERS].reshape(NB, B) / alpha - (sine * alpha / rho) * search
+    pltpu.make_async_copy(others, others, b_ssem).wait()
 
 
 def per_device(blocks, block_rows, block_cols, counts, data):
@@ -361,6 +372,8 @@
             pltpu.VMEM((ITERS, NY, HALF + 1, B), F32),
             pltpu.VMEM((1, B), F32),
             pltpu.VMEM((N_COL, 1, B), F32),
+            pltpu.VMEM((1, B), F32),
+            pltpu.VMEM((N_ROW, 1, B), F32),
             pltpu.VMEM((ITERS + 1, 8, B), F32),
             pltpu.SemaphoreType.DMA((3,)),
             pltpu.SemaphoreType.DMA((LOADS,)),
@@ -374,6 +387,8 @@
             pltpu.SemaphoreType.DMA((ITERS,)),
             pltpu.SemaphoreType.DMA,
             pltpu.SemaphoreType.DMA((ITERS,)),
+            pltpu.SemaphoreType.DMA,
+            pltpu.SemaphoreType.DMA,
             pltpu.SemaphoreType.DMA,
             pltpu.SemaphoreType.DMA,
         ],

time: 98.5 us -> 98 us (level)
  no operation moved by 1% of the time
where the time goes in v7:
time: 98 us; the launch traced here: 97.9 us
  Pallas kernels  95.8 us (98%)
  between operations  1.29 us (1%)
    pallas_call x1, Pallas kernels, per_device(): pl.pallas_call(kernel, out_shape=jax.ShapeDtypeStruct((3, NB, B), F32), i...  95.8 us

profile of v7, /device:TPU:1, one launch (start us, length us, event | category | flops | bytes accessed | tf_op | source)
XLA Modules:
  0.0 97.9 jit_solution(8003774089947205126)
XLA Ops:
  1.3 95.8 %lsqr.1 = f32[3,256,128]{2,1,0:T(8,128)S(1)} custom-call(bf16[1,1,256,128,128]{4,3,2,1,0:T(8,128)(2,1)} %blocks_hbm.1, s32[1,256]{1,0:T(1,128)} %bitcast.10, s32[1,256]{1,0:T(1,128)} %bitcast.11, s32[1,1]{1,0:T(1,128)S(6)} %copy.8.counts_ref, f32[256,128]{1,0:T(8,128)} %bitcast.9), custom_call_target="tpu_custom_call" | custom-call | tf_op jit(solution)/shard_map/lsqr/pallas_call | solution.py:349
  97.1 0.8 slice_bitcast_fusion

commit v8 on v7

--- a/solution.py
+++ b/solution.py
@@ -19,6 +19,8 @@
 LOADS = 4
 HALF = NB // NC
 GROUP = 16
+NEAR = NZ // 2
+HALF_OWNERS = N_ROW // 2
 
 
 def ring(step, size):
@@ -81,41 +83,35 @@
     return mixed + swap_lanes(mixed)
 
 
-def half_adjoint_products(blocks_ref, h, picks, out_ref, add):
-    row = lax.broadcasted_iota(jnp.int32, (GROUP, B), 0)
-    side = jnp.where(left_lanes(GROUP), 0, 1)
-    half = GROUP // 2
-    rows = pl.ds(pl.multiple_of(h * (B // 2), B // 2), B // 2)
-    for g in range(NB // GROUP):
-        base = g * GROUP
-        mine = picks[base : base + GROUP]
-        lhs = jnp.concatenate(
-            [jnp.where((row & (half - 1)) == q + side, mine, 0.0).astype(BF16) for q in range(0, half, 2)], axis=1
-        )
-        left = jnp.concatenate([blocks_ref[base + q, rows] for q in range(half)], axis=0)
-        right = jnp.concatenate([blocks_ref[base + half + q, rows] for q in range(half)], axis=0)
-        res = jnp.dot(lhs, jnp.concatenate([left, right], axis=1), preferred_element_type=F32)
-        res = jnp.where(row < half, res[:, :B], res[:, B:])
-        if add:
-            res = res + out_ref[base : base + GROUP, :]
-        out_ref[base : base + GROUP, :] = res
-
-
-def half_forward_products(blk_t, h, picks, out_ref):
+def quarter_products(store, hn, hk, picks, out_ref, add):
     wide = 2 * GROUP
     row = lax.broadcasted_iota(jnp.int32, (wide, B), 0)
-    keep = ((lax.broadcasted_iota(jnp.int32, (GROUP, B), 0) < 8) & left_lanes(GROUP)) | (
-        (lax.broadcasted_iota(jnp.int32, (GROUP, B), 0) >= 8) & ~left_lanes(GROUP)
-    )
+    side = jnp.where(left_lanes(wide), 0, 1)
+    upper = lax.broadcasted_iota(jnp.int32, (GROUP, B), 0) < 8
+    keep = (upper & left_lanes(GROUP)) | (~upper & ~left_lanes(GROUP))
+    rows = pl.ds(pl.multiple_of(hk * (B // 2), B // 2), B // 2)
     for g in range(NB // wide):
         base = g * wide
         mine = picks[base : base + wide]
-        lhs = jnp.concatenate([jnp.where((row & 7) == q, mine, 0.0).astype(BF16) for q in range(8)], axis=1)
-        left = jnp.concatenate([blk_t[h, (g * 8 + q) * 2] for q in range(8)], axis=0)
-        right = jnp.concatenate([blk_t[h, (g * 8 + q) * 2 + 1] for q in range(8)], axis=0)
+        lhs = jnp.concatenate(
+            [jnp.where((row & 7) == q + side, mine, 0.0).astype(BF16) for q in range(0, 8, 2)], axis=1
+        )
+        left = jnp.concatenate([store[hn, (g * 8 + q) * 2, rows] for q in range(8)], axis=0)
+        right = jnp.concatenate([store[hn, (g * 8 + q) * 2 + 1, rows] for q in range(8)], axis=0)
         res = jnp.dot(lhs, jnp.concatenate([left, right], axis=1), preferred_element_type=F32)
-        out_ref[base : base + GROUP, :] = jnp.where(keep, res[:GROUP, :B], 0.0)
-        out_ref[base + GROUP : base + wide, :] = jnp.where(keep, res[GROUP:, B:], 0.0)
+        low = jnp.where(keep, res[:GROUP, :B], 0.0)
+        high = jnp.where(keep, res[GROUP:, B:], 0.0)
+        if add:
+            low = low + out_ref[base : base + GROUP, :]
+            high = high + out_ref[base + GROUP : base + wide, :]
+        out_ref[base : base + GROUP, :] = low
+        out_ref[base + GROUP : base + wide, :] = high
+
+
+def scatter_half(place, prod):
+    both = scatter_rows(place, prod)
+    both = both + swap_lanes(both)
+    return jnp.where(left_lanes(HALF), both[:HALF], both[HALF:])
 
 
 def pick_rows(pick, vector):
@@ -141,7 +137,7 @@
 def kernel(
     blocks_hbm, rows_hbm, cols_hbm, counts_ref, data_hbm,
     out,
-    blk, blk_t, rows_v, cols_v, pick_r, pick_c, place_r, place_c, prod,
+    blk, blk_t, blk_n, rows_v, cols_v, pick_r, pick_c, place_r, place_c, prod, prod_b,
     data, tb, wb, gsend, grecv, fsend, frecv, psend, precv, asend, arecv, bsend, brecv, scal,
     in_sem, blk_sem, g_ssem, g_rsem, w_ssem, w_rsem, f_ssem, f_rsem, p_ssem, p_rsem, t_ssem, t_rsem, a_ssem, a_rsem, b_ssem, b_rsem,
 ):
@@ -149,7 +145,17 @@
     c = lax.axis_index("col")
     x, z = r // NZ, r % NZ
     y, core = c // NC, c % NC
-    row_peers = [((x + dx) % NX) * NZ + (z + dz) % NZ for dx, dz in ROW_STEPS]
+    row_xz = [((x + dx) % NX, (z + dz) % NZ) for dx, dz in ROW_STEPS]
+    row_peers = [px * NZ + pz for px, pz in row_xz]
+    near = z // NEAR
+    steps = [(dx, dz) for dx in (2, 1, 3, 0) for dz in range(NEAR)]
+    far_xz = [((x + dx) % NX, (1 - near) * NEAR + (z + dz) % NEAR) for dx, dz in steps]
+    near_xz = [((x + dx) % NX, near * NEAR + (z + dz) % NEAR) for dx, dz in steps if dx or dz]
+
+    def chunk_of(px, pz):
+        return (pz // NEAR) * HALF_OWNERS + px * NEAR + pz % NEAR
+
+    own = chunk_of(x, z)
     twin = y * NC + 1 - core
     y_peers = [((y + dy) % NY) * NC + core for dy in (2, 1, 3)]
     col_peers = [((y + dy) % NY) * NC + (core + dc) % NC for dy, dc in COL_STEPS]
@@ -194,20 +200,32 @@
     pick_c[...] = hot_c.T.astype(BF16)
     place_c[...] = jnp.where(live, hot_c, 0.0).astype(BF16)
 
-    def adjoint_place(squares):
-        part = scatter_rows(place_c[...], prod[...])
-        gsend[:, :RCH, :] = part.reshape(N_ROW, RCH, B)
+    def send_to_owners(it, owners):
+        for px, pz in owners:
+            pltpu.make_async_remote_copy(
+                gsend.at[chunk_of(px, pz)], grecv.at[it, r], g_ssem, g_rsem.at[it],
+                device_id=(px * NZ + pz, c), device_id_type=MESH,
+            ).start()
+
+    def put_squares(squares):
         gsend[:, RCH:, :] = jnp.broadcast_to(squares.reshape(1, 1, B), (N_ROW, 1, B))
 
-    def start_adjoint_send(it):
-        for p in row_peers:
-            pltpu.make_async_remote_copy(
-                gsend.at[p], grecv.at[it, r], g_ssem, g_rsem.at[it], device_id=(p, c), device_id_type=MESH
-            ).start()
-        grecv[it, r] = gsend[r]
+    def put_half(h, packed):
+        gsend[pl.ds(h * HALF_OWNERS, HALF_OWNERS), :RCH, :] = packed.reshape(HALF_OWNERS, RCH, B)
+
+    def model_half(it, h):
+        return wb[it, pl.ds(h * HALF_OWNERS, HALF_OWNERS)].reshape(HALF, B)
+
+    def wait_chunks(it, which):
+        landed = wb.at[it, pl.ds(0, HALF_OWNERS - 1 + which)]
+        pltpu.make_async_copy(landed, landed, w_rsem.at[it, which]).wait()
+
+    def wait_chunks_sent(it):
+        sent = wb.at[it, pl.ds(0, N_ROW - 1)]
+        pltpu.make_async_copy(sent, sent, w_ssem).wait()
 
     def start_last_norm():
-        asend[...] = lane_squares(wb[ITERS, r])
+        asend[...] = lane_squares(wb[ITERS, own])
         for p in col_peers:
             pltpu.make_async_remote_copy(
                 asend, arecv.at[c], a_ssem, a_rsem, device_id=(r, p), device_id_type=MESH
@@ -224,7 +242,7 @@
         pltpu.make_async_copy(others, others, a_ssem).wait()
 
     def finish_adjoint(it, first):
-        before = None if first else wb[it - 1, r] / scal[it - 1, 0:1, 0:1]
+        before = None if first else wb[it - 1, own] / scal[it - 1, 0:1, 0:1]
         got = grecv.at[it, pl.ds(0, N_ROW - 1)]
         pltpu.make_async_copy(got, got, g_rsem.at[it]).wait()
         total = jnp.sum(grecv[it], axis=0)
@@ -232,36 +250,38 @@
         chunk = total[:RCH] / beta
         if not first:
             chunk = chunk - beta * before
-        wb[it, r] = chunk
+        wb[it, own] = chunk
         scal[it, 1:2, :] = jnp.broadcast_to(beta, (1, B))
-        for p in row_peers:
+        for px, pz in row_xz:
             pltpu.make_async_remote_copy(
-                wb.at[it, r], wb.at[it, r], w_ssem, w_rsem.at[it], device_id=(p, c), device_id_type=MESH
+                wb.at[it, own], wb.at[it, own], w_ssem, w_rsem.at[it, (pz // NEAR + near) % 2],
+                device_id=(px * NZ + pz, c), device_id_type=MESH,
             ).start()
         if not first:
             pl.when(it == ITERS)(start_last_norm)
         pltpu.make_async_copy(got, got, g_ssem).wait()
-        landed = wb.at[it, pl.ds(0, N_ROW - 1)]
-        pltpu.make_async_copy(landed, landed, w_rsem.at[it]).wait()
-        pltpu.make_async_copy(landed, landed, w_ssem).wait()
-
-    def forward_half(h, picks):
-        half_forward_products(blk_t, h, picks, prod)
-        both = scatter_rows(place_r[...], prod[...])
-        both = both + swap_lanes(both)
-        return jnp.where(left_lanes(HALF), both[:HALF], both[HALF:])
 
     def forward_and_adjoint(it):
-        vec = wb[it].reshape(NB, B)
-        picks = pick_rows(pick_c[...], vec)
-        squares = lane_squares(vec)
-        fsend[:HALF, :] = forward_half(1 - core, picks)
+        wait_chunks(it, 0)
+        part = model_half(it, near)
+        picks = pick_half(pick_c[...], part)
+        quarter_products(blk_t, 1 - core, near, picks, prod, False)
+        quarter_products(blk_t, core, near, picks, prod_b, False)
+        squares = lane_squares(part)
+        wait_chunks(it, 1)
+        part = model_half(it, 1 - near)
+        picks = pick_half(pick_c[...], part)
+        quarter_products(blk_t, 1 - core, 1 - near, picks, prod, True)
+        both = lane_squares(part)
+        squares = jnp.where(near == 0, squares, both) + jnp.where(near == 0, both, squares)
+        fsend[:HALF, :] = scatter_half(place_r[...], prod[...])
         fsend[HALF:, :] = squares
         pair = pltpu.make_async_remote_copy(
             fsend, frecv.at[it], f_ssem, f_rsem.at[it], device_id=(r, twin), device_id_type=MESH
         )
         pair.start()
-        psend[:HALF, :] = forward_half(core, picks)
+        quarter_products(blk_t, core, 1 - near, picks, prod_b, True)
+        psend[:HALF, :] = scatter_half(place_r[...], prod_b[...])
         psend[HALF:, :] = squares
         pair.wait()
         psend[...] = psend[...] + frecv[it]
@@ -282,31 +302,56 @@
         )
         done.start()
         scal[it, 0:1, :] = jnp.broadcast_to(alpha, (1, B))
-        half_adjoint_products(blk, core, pick_half(pick_r[...], tb[it + 1, core]), prod, False)
+        picks = pick_half(pick_r[...], tb[it + 1, core])
+        quarter_products(blk_n, 1 - near, core, picks, prod, False)
+        quarter_products(blk_n, near, core, picks, prod_b, False)
         pltpu.make_async_copy(got, got, p_ssem).wait()
+        wait_chunks_sent(it)
         done.wait()
-        half_adjoint_products(blk, 1 - core, pick_half(pick_r[...], tb[it + 1, 1 - core]), prod, True)
-        adjoint_place(lane_squares(tb[it + 1, 0]) + lane_squares(tb[it + 1, 1]))
+        picks = pick_half(pick_r[...], tb[it + 1, 1 - core])
+        quarter_products(blk_n, 1 - near, 1 - core, picks, prod, True)
+        put_squares(lane_squares(tb[it + 1, 0]) + lane_squares(tb[it + 1, 1]))
+        put_half(1 - near, scatter_half(place_c[...], prod[...]))
+        send_to_owners(it + 1, far_xz)
+        quarter_products(blk_n, near, 1 - core, picks, prod_b, True)
+        put_half(near, scatter_half(place_c[...], prod_b[...]))
+        send_to_owners(it + 1, near_xz)
+        grecv[it + 1, r] = gsend[own]
 
     block_products(blk, pick_rows(pick_r[...], data[...]), prod, loads)
-    adjoint_place(lane_squares(data[...]))
+    first, second = halves(scatter_rows(place_c[...], prod[...]))
+    put_half(0, first)
+    put_half(1, second)
+    put_squares(lane_squares(data[...]))
     pl.semaphore_wait(barrier, N_ROW + N_COL - 2)
-    start_adjoint_send(0)
+    send_to_owners(0, row_xz)
+    grecv[0, r] = gsend[own]
     tb[0, 0], tb[0, 1] = halves(data[...])
 
+    def pair_of(n):
+        return (n // 16) * 32 + (n % 2) * 16 + (n // 2) % 8
+
     def transpose_pair(n, carry):
-        first = (n // 16) * 32 + (n % 2) * 16 + (n // 2) % 8
+        k = pair_of(n)
         for h in range(2):
             rows = slice(h * (B // 2), (h + 1) * (B // 2))
-            blk_t[h, n] = jnp.concatenate([blk[first, rows], blk[first + 8, rows]], axis=0).T
+            blk_t[h, n] = jnp.concatenate([blk[k, rows], blk[k + 8, rows]], axis=0).T
+        return carry
+
+    def repack_pair(n, carry):
+        k = pair_of(n)
+        one, two = blk[k], blk[k + 8]
+        half = B // 2
+        blk_n[0, n] = jnp.concatenate([one[:, :half], two[:, :half]], axis=1)
+        blk_n[1, n] = jnp.concatenate([one[:, half:], two[:, half:]], axis=1)
         return carry
 
     lax.fori_loop(0, NB // 2, transpose_pair, 0, unroll=8)
     finish_adjoint(0, True)
+    lax.fori_loop(0, NB // 2, repack_pair, 0, unroll=8)
 
     def step(it, carry):
         forward_and_adjoint(it)
-        start_adjoint_send(it + 1)
         finish_adjoint(it + 1, False)
         return carry
 
@@ -317,6 +362,9 @@
     top, bottom = whole(tb[ITERS, 0] / betas[ITERS], tb[ITERS, 1] / betas[ITERS])
     out[2, :HALF] = top
     out[2, HALF:] = bottom
+    wait_chunks(ITERS, 0)
+    wait_chunks(ITERS, 1)
+    wait_chunks_sent(ITERS)
     search = wb[0].reshape(NB, B) / alphas[0]
     answer = jnp.zeros((NB, B), F32)
     phibar, rhobar = betas[0], alphas[0]
@@ -331,11 +379,16 @@
             theta = sine * alphas[i + 1]
             rhobar = -cosine * alphas[i + 1]
             search = wb[i + 1].reshape(NB, B) / alphas[i + 1] - (theta / rho) * search
-    out[0] = answer
+    top, bottom = whole(answer[:HALF], answer[HALF:])
+    out[0, :HALF] = top
+    out[0, HALF:] = bottom
     others = brecv.at[pl.ds(0, N_ROW - 1)]
     pltpu.make_async_copy(others, others, b_rsem).wait()
     alpha = norm_of(jnp.sum(brecv[...], axis=0))
-    out[1] = wb[ITERS].reshape(NB, B) / alpha - (sine * alpha / rho) * search
+    search = wb[ITERS].reshape(NB, B) / alpha - (sine * alpha / rho) * search
+    top, bottom = whole(search[:HALF], search[HALF:])
+    out[1, :HALF] = top
+    out[1, HALF:] = bottom
     pltpu.make_async_copy(others, others, b_ssem).wait()
 
 
@@ -354,12 +407,14 @@
         scratch_shapes=[
             pltpu.VMEM((NB, B, B), BF16),
             pltpu.VMEM((2, NB // 2, B, B), BF16),
+            pltpu.VMEM((2, NB // 2, B, B), BF16),
             pltpu.VMEM((1, NB), jnp.int32),
             pltpu.VMEM((1, NB), jnp.int32),
             pltpu.VMEM((NB, NB), BF16),
             pltpu.VMEM((NB, NB), BF16),
             pltpu.VMEM((NB, NB), BF16),
             pltpu.VMEM((NB, NB), BF16),
+            pltpu.VMEM((NB, B), F32),
             pltpu.VMEM((NB, B), F32),
             pltpu.VMEM((NB, B), F32),
             pltpu.VMEM((ITERS + 1, 2, HALF, B), F32),
@@ -380,7 +435,7 @@
             pltpu.SemaphoreType.DMA,
             pltpu.SemaphoreType.DMA((ITERS + 1,)),
             pltpu.SemaphoreType.DMA,
-            pltpu.SemaphoreType.DMA((ITERS + 1,)),
+            pltpu.SemaphoreType.DMA((ITERS + 1, 2)),
             pltpu.SemaphoreType.DMA,
             pltpu.SemaphoreType.DMA((ITERS,)),
             pltpu.SemaphoreType.DMA,

time: 98 us -> 98.8 us (level)
  no operation moved by 1% of the time
where the time goes in v8:
time: 98.8 us; the launch traced here: 98.7 us
  Pallas kernels  96.6 us (98%)
  between operations  1.29 us (1%)
    pallas_call x1, Pallas kernels, per_device(): pl.pallas_call(kernel, out_shape=jax.ShapeDtypeStruct((3, NB, B), F32), i...  96.6 us

profile of v8, /device:TPU:1, one launch (start us, length us, event | category | flops | bytes accessed | tf_op | source)
XLA Modules:
  0.0 98.7 jit_solution(9063308011143964793)
XLA Ops:
  1.3 96.6 %lsqr.1 = f32[3,256,128]{2,1,0:T(8,128)S(1)} custom-call(bf16[1,1,256,128,128]{4,3,2,1,0:T(8,128)(2,1)} %blocks_hbm.1, s32[1,256]{1,0:T(1,128)} %bitcast.10, s32[1,256]{1,0:T(1,128)} %bitcast.11, s32[1,1]{1,0:T(1,128)S(6)} %copy.8.counts_ref, f32[256,128]{1,0:T(8,128)} %bitcast.9), custom_call_target="tpu_custom_call" | custom-call | tf_op jit(solution)/shard_map/lsqr/pallas_call | solution.py:402
  97.9 0.8 slice_bitcast_fusion

commit v9 on v8

--- a/solution.py
+++ b/solution.py
@@ -83,6 +83,26 @@
     return mixed + swap_lanes(mixed)
 
 
+def half_adjoint_products(blocks_ref, h, picks, out_ref, add):
+    row = lax.broadcasted_iota(jnp.int32, (GROUP, B), 0)
+    side = jnp.where(left_lanes(GROUP), 0, 1)
+    half = GROUP // 2
+    rows = pl.ds(pl.multiple_of(h * (B // 2), B // 2), B // 2)
+    for g in range(NB // GROUP):
+        base = g * GROUP
+        mine = picks[base : base + GROUP]
+        lhs = jnp.concatenate(
+            [jnp.where((row & (half - 1)) == q + side, mine, 0.0).astype(BF16) for q in range(0, half, 2)], axis=1
+        )
+        left = jnp.concatenate([blocks_ref[base + q, rows] for q in range(half)], axis=0)
+        right = jnp.concatenate([blocks_ref[base + half + q, rows] for q in range(half)], axis=0)
+        res = jnp.dot(lhs, jnp.concatenate([left, right], axis=1), preferred_element_type=F32)
+        res = jnp.where(row < half, res[:, :B], res[:, B:])
+        if add:
+            res = res + out_ref[base : base + GROUP, :]
+        out_ref[base : base + GROUP, :] = res
+
+
 def quarter_products(store, hn, hk, picks, out_ref, add):
     wide = 2 * GROUP
     row = lax.broadcasted_iota(jnp.int32, (wide, B), 0)
@@ -137,7 +157,7 @@
 def kernel(
     blocks_hbm, rows_hbm, cols_hbm, counts_ref, data_hbm,
     out,
-    blk, blk_t, blk_n, rows_v, cols_v, pick_r, pick_c, place_r, place_c, prod, prod_b,
+    blk, blk_t, rows_v, cols_v, pick_r, pick_c, place_r, place_c, prod, prod_b,
     data, tb, wb, gsend, grecv, fsend, frecv, psend, precv, asend, arecv, bsend, brecv, scal,
     in_sem, blk_sem, g_ssem, g_rsem, w_ssem, w_rsem, f_ssem, f_rsem, p_ssem, p_rsem, t_ssem, t_rsem, a_ssem, a_rsem, b_ssem, b_rsem,
 ):
@@ -148,9 +168,6 @@
     row_xz = [((x + dx) % NX, (z + dz) % NZ) for dx, dz in ROW_STEPS]
     row_peers = [px * NZ + pz for px, pz in row_xz]
     near = z // NEAR
-    steps = [(dx, dz) for dx in (2, 1, 3, 0) for dz in range(NEAR)]
-    far_xz = [((x + dx) % NX, (1 - near) * NEAR + (z + dz) % NEAR) for dx, dz in steps]
-    near_xz = [((x + dx) % NX, near * NEAR + (z + dz) % NEAR) for dx, dz in steps if dx or dz]
 
     def chunk_of(px, pz):
         return (pz // NEAR) * HALF_OWNERS + px * NEAR + pz % NEAR
@@ -200,18 +217,19 @@
     pick_c[...] = hot_c.T.astype(BF16)
     place_c[...] = jnp.where(live, hot_c, 0.0).astype(BF16)
 
-    def send_to_owners(it, owners):
-        for px, pz in owners:
+    def put_parts(squares):
+        parts = halves(scatter_rows(place_c[...], prod[...]))
+        for h in range(2):
+            gsend[h * HALF_OWNERS : (h + 1) * HALF_OWNERS, :RCH, :] = parts[h].reshape(HALF_OWNERS, RCH, B)
+        gsend[:, RCH:, :] = jnp.broadcast_to(squares.reshape(1, 1, B), (N_ROW, 1, B))
+
+    def send_to_owners(it):
+        for px, pz in row_xz:
             pltpu.make_async_remote_copy(
                 gsend.at[chunk_of(px, pz)], grecv.at[it, r], g_ssem, g_rsem.at[it],
                 device_id=(px * NZ + pz, c), device_id_type=MESH,
             ).start()
-
-    def put_squares(squares):
-        gsend[:, RCH:, :] = jnp.broadcast_to(squares.reshape(1, 1, B), (N_ROW, 1, B))
-
-    def put_half(h, packed):
-        gsend[pl.ds(h * HALF_OWNERS, HALF_OWNERS), :RCH, :] = packed.reshape(HALF_OWNERS, RCH, B)
+        grecv[it, r] = gsend[own]
 
     def model_half(it, h):
         return wb[it, pl.ds(h * HALF_OWNERS, HALF_OWNERS)].reshape(HALF, B)
@@ -303,29 +321,21 @@
         done.start()
         scal[it, 0:1, :] = jnp.broadcast_to(alpha, (1, B))
         picks = pick_half(pick_r[...], tb[it + 1, core])
-        quarter_products(blk_n, 1 - near, core, picks, prod, False)
-        quarter_products(blk_n, near, core, picks, prod_b, False)
+        half_adjoint_products(blk, core, picks, prod, False)
         pltpu.make_async_copy(got, got, p_ssem).wait()
         wait_chunks_sent(it)
+        squares = lane_squares(tb[it + 1, core])
         done.wait()
-        picks = pick_half(pick_r[...], tb[it + 1, 1 - core])
-        quarter_products(blk_n, 1 - near, 1 - core, picks, prod, True)
-        put_squares(lane_squares(tb[it + 1, 0]) + lane_squares(tb[it + 1, 1]))
-        put_half(1 - near, scatter_half(place_c[...], prod[...]))
-        send_to_owners(it + 1, far_xz)
-        quarter_products(blk_n, near, 1 - core, picks, prod_b, True)
-        put_half(near, scatter_half(place_c[...], prod_b[...]))
-        send_to_owners(it + 1, near_xz)
-        grecv[it + 1, r] = gsend[own]
+        other = tb[it + 1, 1 - core]
+        half_adjoint_products(blk, 1 - core, pick_half(pick_r[...], other), prod, True)
+        both = lane_squares(other)
+        put_parts(jnp.where(core == 0, squares, both) + jnp.where(core == 0, both, squares))
+        send_to_owners(it + 1)
 
     block_products(blk, pick_rows(pick_r[...], data[...]), prod, loads)
-    first, second = halves(scatter_rows(place_c[...], prod[...]))
-    put_half(0, first)
-    put_half(1, second)
-    put_squares(lane_squares(data[...]))
+    put_parts(lane_squares(data[...]))
     pl.semaphore_wait(barrier, N_ROW + N_COL - 2)
-    send_to_owners(0, row_xz)
-    grecv[0, r] = gsend[own]
+    send_to_owners(0)
     tb[0, 0], tb[0, 1] = halves(data[...])
 
     def pair_of(n):
@@ -338,17 +348,8 @@
             blk_t[h, n] = jnp.concatenate([blk[k, rows], blk[k + 8, rows]], axis=0).T
         return carry
 
-    def repack_pair(n, carry):
-        k = pair_of(n)
-        one, two = blk[k], blk[k + 8]
-        half = B // 2
-        blk_n[0, n] = jnp.concatenate([one[:, :half], two[:, :half]], axis=1)
-        blk_n[1, n] = jnp.concatenate([one[:, half:], two[:, half:]], axis=1)
-        return carry
-
     lax.fori_loop(0, NB // 2, transpose_pair, 0, unroll=8)
     finish_adjoint(0, True)
-    lax.fori_loop(0, NB // 2, repack_pair, 0, unroll=8)
 
     def step(it, carry):
         forward_and_adjoint(it)
@@ -407,7 +408,6 @@
         scratch_shapes=[
             pltpu.VMEM((NB, B, B), BF16),
             pltpu.VMEM((2, NB // 2, B, B), BF16),
-            pltpu.VMEM((2, NB // 2, B, B), BF16),
             pltpu.VMEM((1, NB), jnp.int32),
             pltpu.VMEM((1, NB), jnp.int32),
             pltpu.VMEM((NB, NB), BF16),

time: 98.8 us -> 98.6 us (level)
  no operation moved by 1% of the time
where the time goes in v9:
time: 98.6 us; the launch traced here: 98.5 us
  Pallas kernels  96.5 us (98%)
  between operations  1.29 us (1%)
    pallas_call x1, Pallas kernels, per_device(): pl.pallas_call(kernel, out_shape=jax.ShapeDtypeStruct((3, NB, B), F32), i...  96.5 us

profile of v9, /device:TPU:1, one launch (start us, length us, event | category | flops | bytes accessed | tf_op | source)
XLA Modules:
  0.0 98.5 jit_solution(2259233987420163499)
XLA Ops:
  1.3 96.5 %lsqr.1 = f32[3,256,128]{2,1,0:T(8,128)S(1)} custom-call(bf16[1,1,256,128,128]{4,3,2,1,0:T(8,128)(2,1)} %blocks_hbm.1, s32[1,256]{1,0:T(1,128)} %bitcast.10, s32[1,256]{1,0:T(1,128)} %bitcast.11, s32[1,1]{1,0:T(1,128)S(6)} %copy.8.counts_ref, f32[256,128]{1,0:T(8,128)} %bitcast.9), custom_call_target="tpu_custom_call" | custom-call | tf_op jit(solution)/shard_map/lsqr/pallas_call | solution.py:403
  97.8 0.8 slice_bitcast_fusion

commit v10 on v7

--- a/solution.py
+++ b/solution.py
@@ -27,7 +27,7 @@
 
 ROW_STEPS = sorted(
     ((dx, dz) for dx in range(NX) for dz in range(NZ) if dx or dz),
-    key=lambda s: -(ring(s[0], NX) + ring(s[1], NZ)),
+    key=lambda s: (-(ring(s[0], NX) + ring(s[1], NZ)), s[1], s[0]),
 )
 
 COL_STEPS = sorted(

time: 98 us -> 97.7 us (level)
  no operation moved by 1% of the time
where the time goes in v10:
time: 97.7 us; the launch traced here: 97.6 us
  Pallas kernels  95.6 us (98%)
  between operations  1.29 us (1%)
    pallas_call x1, Pallas kernels, per_device(): pl.pallas_call(kernel, out_shape=jax.ShapeDtypeStruct((3, NB, B), F32), i...  95.6 us

profile of v10, /device:TPU:1, one launch (start us, length us, event | category | flops | bytes accessed | tf_op | source)
XLA Modules:
  0.0 97.6 jit_solution(12146131823163492873)
XLA Ops:
  1.3 95.6 %lsqr.1 = f32[3,256,128]{2,1,0:T(8,128)S(1)} custom-call(bf16[1,1,256,128,128]{4,3,2,1,0:T(8,128)(2,1)} %blocks_hbm.1, s32[1,256]{1,0:T(1,128)} %bitcast.10, s32[1,256]{1,0:T(1,128)} %bitcast.11, s32[1,1]{1,0:T(1,128)S(6)} %copy.8.counts_ref, f32[256,128]{1,0:T(8,128)} %bitcast.9), custom_call_target="tpu_custom_call" | custom-call | tf_op jit(solution)/shard_map/lsqr/pallas_call | solution.py:349
  96.9 0.8 slice_bitcast_fusion

commit v11 on v7

--- a/solution.py
+++ b/solution.py
@@ -16,7 +16,7 @@
 N_ROW = NX * NZ
 N_COL = NY * NC
 RCH = NB // N_ROW
-LOADS = 4
+LOADS = 8
 HALF = NB // NC
 GROUP = 16
 
@@ -187,12 +187,8 @@
     def one_hot(index_ref):
         return (sub == index_ref[...]).astype(F32)
 
-    hot_r = one_hot(rows_v)
-    pick_r[...] = hot_r.T.astype(BF16)
-    place_r[...] = jnp.where(live, hot_r, 0.0).astype(BF16)
-    hot_c = one_hot(cols_v)
-    pick_c[...] = hot_c.T.astype(BF16)
-    place_c[...] = jnp.where(live, hot_c, 0.0).astype(BF16)
+    pick_r[...] = one_hot(rows_v).T.astype(BF16)
+    place_c[...] = jnp.where(live, one_hot(cols_v), 0.0).astype(BF16)
 
     def adjoint_place(squares):
         part = scatter_rows(place_c[...], prod[...])
@@ -301,6 +297,8 @@
             blk_t[h, n] = jnp.concatenate([blk[first, rows], blk[first + 8, rows]], axis=0).T
         return carry
 
+    pick_c[...] = one_hot(cols_v).T.astype(BF16)
+    place_r[...] = jnp.where(live, one_hot(rows_v), 0.0).astype(BF16)
     lax.fori_loop(0, NB // 2, transpose_pair, 0, unroll=8)
     finish_adjoint(0, True)
 

time: 98 us -> 99.4 us (1.014)
  Pallas kernels: 95.8 us -> 97.2 us
    pallas_call x1, Pallas kernels: 95.8 us -> 97.2 us  [per_device(): pl.pallas_call(kernel, out_shape=jax.ShapeDtypeStruct((3, NB, B), F32), i...]
where the time goes in v11:
time: 99.4 us; the launch traced here: 99.3 us
  Pallas kernels  97.2 us (98%)
  between operations  1.29 us (1%)
    pallas_call x1, Pallas kernels, per_device(): pl.pallas_call(kernel, out_shape=jax.ShapeDtypeStruct((3, NB, B), F32), i...  97.2 us

profile of v11, /device:TPU:1, one launch (start us, length us, event | category | flops | bytes accessed | tf_op | source)
XLA Modules:
  0.0 99.3 jit_solution(11775451495041529652)
XLA Ops:
  1.3 97.2 %lsqr.1 = f32[3,256,128]{2,1,0:T(8,128)S(1)} custom-call(bf16[1,1,256,128,128]{4,3,2,1,0:T(8,128)(2,1)} %blocks_hbm.1, s32[1,256]{1,0:T(1,128)} %bitcast.10, s32[1,256]{1,0:T(1,128)} %bitcast.11, s32[1,1]{1,0:T(1,128)S(6)} %copy.8.counts_ref, f32[256,128]{1,0:T(8,128)} %bitcast.9), custom_call_target="tpu_custom_call" | custom-call | tf_op jit(solution)/shard_map/lsqr/pallas_call | solution.py:347
  98.5 0.8 slice_bitcast_fusion
